TPU v7x, 128 devices: a whole 4x4x4 slice. The times are simulated.
128 devices in a mesh: dp: 2 (over core), expert: 64 (over z, y, x).
Axes of the slice: x: 4, y: 4, z: 4, core: 2. Of those that a mesh axis runs over, the one named last changes fastest.
Arguments:
- tokens: bfloat16 [1536, 5120], P(('dp', 'expert')), may hold values from -6 to 6
- router_weight: bfloat16 [1536], P(('dp', 'expert')), may hold values from 0.19921875 to 1
- initial_id: int32 [1536, 1], P(('dp', 'expert')), may hold values from 0 to 3; in each aligned block of 768 rows (0 to 767, 768 to 1535, ...) at most 320 rows name the same one
- group_map: int32 [4], replicated, may hold values from 0 to 1, as said below
- teacher_gate: bfloat16 [5120, 16384], P(None, 'expert'), may hold values from -0.078125 to 0.078125
- teacher_up: bfloat16 [5120, 16384], P(None, 'expert'), may hold values from -0.078125 to 0.078125
- teacher_down: bfloat16 [16384, 5120], P('expert'), may hold values from -0.09375 to 0.09375
- student_gate: bfloat16 [5120, 8192], P(None, 'expert'), may hold values from -0.078125 to 0.078125
- student_up: bfloat16 [5120, 8192], P(None, 'expert'), may hold values from -0.078125 to 0.078125
- student_down: bfloat16 [8192, 5120], P('expert'), may hold values from -0.09375 to 0.09375
Outputs:
- grad_gate: float32 [5120, 8192], P('dp', 'expert')
- grad_up: float32 [5120, 8192], P('dp', 'expert')
- grad_down: float32 [8192, 5120], P('expert', 'dp')
Inputs may be any that keep to these rules, and one draw needn't show every extreme that they name: `initial_id`: in each half of the tokens (rows h * 12 * 64 to (h + 1) * 12 * 64 - 1, h = 0, 1) every initial expert is named by at most 320 tokens, and some expert of some half by exactly 320. `group_map`: every merged expert is named by exactly 2 entries.
All inputs are finite; a program needn't handle non-finite values.
Results may differ from a plain program's by a relative error of at most 0.013.
Values may be sent and summed in bfloat16 or wider, within the bound.
No kernel may reach another device: no remote copies, remote signals or barrier semaphores. Data moves between devices by JAX's collectives and lax.ppermute only.
A program may use at most 128 MiB of HBM per device.

v0:
```python
import math

import jax
import jax.numpy as jnp
from jax import lax
from jax.sharding import PartitionSpec as P

F = 4096
E_ORIG = 4
GROUP = 2


def pick_rows(ids, target, capacity):
    count = ids.shape[0]
    member = ids == target
    keys = jnp.where(member, 0, 1).astype(jnp.int32) * count + jnp.arange(count, dtype=jnp.int32)
    order = jnp.argsort(keys)[:capacity]
    live = jnp.sum(member.astype(jnp.int32))
    valid = jnp.arange(capacity, dtype=jnp.int32) < live
    return (order, valid)


def expert_forward(rows, w_gate, w_up):
    gate = jnp.dot(rows, w_gate, preferred_element_type=jnp.float32)
    upper = jnp.dot(rows, w_up, preferred_element_type=jnp.float32)
    hidden = (jax.nn.silu(gate) * upper).astype(jnp.bfloat16)
    return (gate, upper, hidden)


def per_device(
    tokens,
    router_weight,
    initial_id,
    group_map,
    teacher_gate,
    teacher_up,
    teacher_down,
    student_gate,
    student_up,
    student_down,
):
    whole, weights, id_rows = (
        lax.all_gather(tokens, "expert", axis=0, tiled=True),
        lax.all_gather(router_weight, "expert", axis=0, tiled=True),
        lax.all_gather(initial_id, "expert", axis=0, tiled=True),
    )
    ids = id_rows[:, 0]
    weight = weights.astype(jnp.float32)
    half_rows = whole.shape[0]
    total_tokens = half_rows * lax.axis_size("dp")
    capacity = half_rows * 5 // (E_ORIG * 3)
    owner = lax.axis_index("expert")
    teacher_width = teacher_gate.shape[1]
    student_width = student_gate.shape[1]
    teacher_expert = owner * teacher_width // F
    student_expert = owner * student_width // F
    teacher_idx, teacher_valid = pick_rows(ids, teacher_expert, capacity)
    teacher_x = whole[teacher_idx]
    _, _, teacher_hidden = expert_forward(teacher_x, teacher_gate, teacher_up)
    teacher_scale = jnp.where(teacher_valid, -weight[teacher_idx], 0.0)
    teacher_part = (
        jnp.dot(teacher_hidden, teacher_down, preferred_element_type=jnp.float32)
        * teacher_scale[:, None]
    )
    member_keys = jnp.where(group_map == student_expert, 0, 1).astype(
        jnp.int32
    ) * E_ORIG + jnp.arange(E_ORIG, dtype=jnp.int32)
    members = jnp.argsort(member_keys)[:GROUP]
    index_list, valid_list = ([], [])
    for position in range(GROUP):
        picked, valid = pick_rows(ids, members[position], capacity)
        index_list.append(picked)
        valid_list.append(valid)
    student_idx = jnp.concatenate(index_list)
    student_valid = jnp.concatenate(valid_list)
    student_x = whole[student_idx]
    gate, upper, student_hidden = expert_forward(student_x, student_gate, student_up)
    student_scale = jnp.where(student_valid, weight[student_idx], 0.0)
    student_part = (
        jnp.dot(student_hidden, student_down, preferred_element_type=jnp.float32)
        * student_scale[:, None]
    )
    partial_sum = jnp.zeros((half_rows, whole.shape[1]), jnp.float32)
    partial_sum = partial_sum.at[teacher_idx].add(teacher_part).at[student_idx].add(student_part)
    factor = 1.0 / math.sqrt(total_tokens)
    mismatch = lax.psum(partial_sum, "expert")
    cotangent = (weight[:, None] * mismatch * factor).astype(jnp.bfloat16)
    chosen = jnp.where(student_valid[:, None], cotangent[student_idx], jnp.zeros((), jnp.bfloat16))
    dhidden = jnp.dot(chosen, student_down.T, preferred_element_type=jnp.float32)
    sigma = jax.nn.sigmoid(gate)
    dgate = (dhidden * upper * sigma * (1.0 + gate * (1.0 - sigma))).astype(jnp.bfloat16)
    dup = (dhidden * jax.nn.silu(gate)).astype(jnp.bfloat16)
    gate_grad = jnp.dot(student_x.T, dgate, preferred_element_type=jnp.float32)
    up_grad = jnp.dot(student_x.T, dup, preferred_element_type=jnp.float32)
    down_grad = jnp.dot(student_hidden.T, chosen, preferred_element_type=jnp.float32)
    return (
        lax.psum_scatter(
            gate_grad.astype(jnp.bfloat16), "dp", scatter_dimension=0, tiled=True
        ).astype(jnp.float32),
        lax.psum_scatter(
            up_grad.astype(jnp.bfloat16), "dp", scatter_dimension=0, tiled=True
        ).astype(jnp.float32),
        lax.psum_scatter(
            down_grad.astype(jnp.bfloat16), "dp", scatter_dimension=1, tiled=True
        ).astype(jnp.float32),
    )


def solution(mesh):
    placed = (
        P(("dp", "expert"), None),
        P(("dp", "expert")),
        P(("dp", "expert"), None),
        P(),
        P(None, "expert"),
        P(None, "expert"),
        P("expert", None),
        P(None, "expert"),
        P(None, "expert"),
        P("expert", None),
    )
    return jax.shard_map(
        per_device,
        mesh=mesh,
        in_specs=placed,
        out_specs=(P("dp", "expert"), P("dp", "expert"), P("expert", "dp")),
        check_vma=False,
    )
```

profile of v0, /device:TPU:1, one launch (start us, length us, event | category | flops | bytes accessed | tf_op | source)
XLA Modules:
  0.0 657.6 jit_solution(2720743627860802634)
XLA Ops:
  10.7 154.3 %all-reduce.1 = bf16[768]{0:T(1024)(128)(2,1)S(1)} all-reduce(bf16[768]{0:T(1024)(128)(2,1)S(1)} %dynamic-update-slice.1), channel_id=1, replica_groups=mesh['dp'=2,'expert'=64] {'expert'}, use_global_device_ids=true, to_apply=%add.1 | all-reduce | flops 768 | bytes 3072
  167.2 10.9 %all-reduce = s32[768]{0:T(1024)S(1)} all-reduce(s32[768]{0:T(1024)S(1)} %bitcast_dynamic-update-slice_fusion), channel_id=1, replica_groups=mesh['dp'=2,'expert'=64] {'expert'}, use_global_device_ids=true, to_apply=%add | all-reduce | flops 768 | bytes 6144
  180.6 4.4 sort.63
  185.0 4.4 sort.64
  189.4 4.4 sort.65
  195.8 2.8 gather_fusion.3
  200.5 12.8 %reshape.204 = bf16[768,5120]{1,0:T(8,128)(2,1)} reshape(bf16[64,12,5120]{2,1,0:T(8,128)(2,1)} %all-gather.3.cloned.1.call-done) | data formatting | bytes 15728640
  213.3 14.1 %gather_fusion.1 = bf16[320,5120]{1,0:T(8,128)(2,1)} fusion(bf16[768,5120]{1,0:T(8,128)(2,1)} %reshape.204, s32[1024]{0:T(1024)S(1)} %pad_clamp_fusion), kind=kCustom, calls=%fused_computation.1 | custom fusion | bytes 6554880 | tf_op jit(solution)/shard_map/gather | solution.py:58
  227.5 18.7 %gather_fusion = bf16[640,5120]{1,0:T(8,128)(2,1)} fusion(bf16[768,5120]{1,0:T(8,128)(2,1)} %reshape.204, s32[1024]{0:T(1024)S(1)} %pad_clamp_fusion.1), kind=kCustom, calls=%fused_computation | custom fusion | bytes 13109760 | tf_op jit(solution)/shard_map/gather | solution.py:76
  246.2 5.2 fusion.23
  251.4 3.0 fusion.22
  257.1 9.0 %convolution_multiply_fusion.1 = f32[320,5120]{1,0:T(8,128)} fusion(bf16[256,5120]{1,0:T(8,128)(2,1)S(1)} %copy-done, f32[320]{0:T(512)S(1)} %negate_select_fusion, bf16[320,5120]{1,0:T(8,128)(2,1)} %gather_fusion.1, bf16[5120,256]{1,0:T(8,128)(2,1)} %param.15, f32[320,256]{1,0:T(8,128)S(1)} %fusion.22), kind=kOutput, calls=%fused_computation.11 | convolution fusion | flops 1679851520 | bytes 15402240 | tf_op jit(solution)/shard_map/dot_general | solution.py:62
  266.1 17.7 %scatter_custom_fusion = f32[768,5120]{1,0:T(8,128)} fusion(s32[320]{0:T(512)S(1)} %compare_select_fusion.1, f32[320,5120]{1,0:T(8,128)} %convolution_multiply_fusion.1, f32[]{:T(128)} %constant.50.clone.1), kind=kCustom, calls=%fused_computation.9 | custom fusion | flops 1638400 | bytes 15729152 | tf_op jit(solution)/shard_map/scatter-add | solution.py:84
  283.8 6.6 %convolution_multiply_fusion = f32[640,5120]{1,0:T(8,128)} fusion(bf16[640,128]{1,0:T(8,128)(2,1)S(1)} %get-tuple-element.23, bf16[128,5120]{1,0:T(8,128)(2,1)S(1)} %copy-done.4, f32[640]{0:T(1024)S(1)} %broadcast_select_fusion.3), kind=kOutput, calls=%fused_computation.8 | convolution fusion | flops 842137600 | bytes 14584320 | tf_op jit(solution)/shard_map/dot_general | solution.py:80
  290.4 43.9 %scatter_fusion = f32[768,5120]{1,0:T(8,128)} fusion(f32[768,5120]{1,0:T(8,128)} %scatter_custom_fusion, s32[640]{0:T(1024)S(1)} %fusion.13, f32[640,5120]{1,0:T(8,128)} %convolution_multiply_fusion), kind=kCustom, calls=%fused_computation.6 | custom fusion | flops 3276800 | bytes 39324160 | tf_op jit(solution)/shard_map/scatter-add | solution.py:84
  334.5 238.7 %all-reduce.4.cloned.1.call-done = f32[768,5120]{1,0:T(8,128)} async-done(((f32[768,5120]{1,0:T(8,128)}), f32[768,5120]{1,0:T(8,128)}) %all-reduce.4.cloned.1.call-update) | async-done | bytes 15728656 | tf_op jit(solution)/shard_map/psum | solution.py:86
  573.2 9.0 %multiply_convert_fusion = bf16[768,5120]{1,0:T(8,128)(2,1)} fusion(f32[768,5120]{1,0:T(8,128)} %all-reduce.4.cloned.1.call-done, f32[768]{0:T(1024)S(1)} %convert_element_type.50), kind=kLoop, calls=%fused_computation.7 | loop fusion | flops 11796480 | bytes 23596032 | tf_op jit(solution)/shard_map/convert_element_type | solution.py:87
  582.2 18.5 %gather_fusion.4 = bf16[640,5120]{1,0:T(8,128)(2,1)} fusion(bf16[768,5120]{1,0:T(8,128)(2,1)} %multiply_convert_fusion, s32[1024]{0:T(1024)S(1)} %pad_clamp_fusion.1), kind=kCustom, calls=%fused_computation.4 | custom fusion | bytes 13109760 | tf_op jit(solution)/shard_map/gather | solution.py:88
  600.7 5.2 convolution_convert_fusion
  606.0 4.8 fusion.2
  610.8 5.8 convolution_convert_fusion.2
  616.9 6.1 convolution_convert_fusion.1
  625.4 8.1 %reduce-scatter.4.cloned.1.call-done = bf16[2560,128]{1,0:T(8,128)(2,1)} async-done(((bf16[5120,128]{1,0:T(8,128)(2,1)}), bf16[2560,128]{1,0:T(8,128)(2,1)}) %reduce-scatter.4.cloned.1.call-update) | async-done | bytes 655376 | tf_op jit(solution)/shard_map/reduce_scatter | solution.py:97
  635.7 12.8 %reduce-scatter.6.cloned.1.call-done = bf16[2560,128]{1,0:T(8,128)(2,1)} async-done(((bf16[5120,128]{1,0:T(8,128)(2,1)}), bf16[2560,128]{1,0:T(8,128)(2,1)}) %reduce-scatter.6.cloned.1.call-update) | async-done | bytes 655376 | tf_op jit(solution)/shard_map/reduce_scatter | solution.py:100
  (59 shorter events, 21.4 us)
Async XLA Ops:
  7.2 249.9 %copy-start = (bf16[256,5120]{1,0:T(8,128)(2,1)S(1)}, bf16[256,5120]{1,0:T(8,128)(2,1)}, u32[]{:S(2)}) copy-start(bf16[256,5120]{1,0:T(8,128)(2,1)} %param.16) | copy-start | bytes 7864324
  7.2 193.3 %all-gather.3.cloned.1.call-start = ((), (), s32[]{:S(2)}) async-start(), calls=%async_computation.7 | async-start | bytes 10649600 | tf_op jit(solution)/shard_map/all_gather | solution.py:43
  7.9 565.3 %all-reduce.4.cloned.1.call-start = ((), (), s32[]{:S(2)}) async-start(), calls=%async_computation.3 | async-start | bytes 31457280 | tf_op jit(solution)/shard_map/psum | solution.py:86
  246.2 5.2 copy-start.2
  246.2 8.3 %copy-start.3 = (bf16[640,5120]{1,0:T(8,128)(2,1)S(1)}, bf16[640,5120]{1,0:T(8,128)(2,1)}, u32[]{:S(2)}) copy-start(bf16[640,5120]{1,0:T(8,128)(2,1)} %gather_fusion) | copy-start | bytes 19660804
  246.2 8.3 %copy-start.5 = (bf16[5120,128]{1,0:T(8,128)(2,1)S(1)}, bf16[5120,128]{1,0:T(8,128)(2,1)}, u32[]{:S(2)}) copy-start(bf16[5120,128]{1,0:T(8,128)(2,1)} %param.18) | copy-start | bytes 3932164
  266.1 17.7 %copy-start.4 = (bf16[128,5120]{1,0:T(8,128)(2,1)S(1)}, bf16[128,5120]{1,0:T(8,128)(2,1)}, u32[]{:S(2)}) copy-start(bf16[128,5120]{1,0:T(8,128)(2,1)} %param.19) | copy-start | bytes 3932164
  334.4 288.7 %reduce-scatter.8.cloned.1.call-start = ((), (), s32[]{:S(2)}) async-start(), calls=%async_computation.6 | async-start | bytes 1966080 | tf_op jit(solution)/shard_map/reduce_scatter | solution.py:103
  605.9 4.9 copy-start.6
  605.9 27.6 %reduce-scatter.4.cloned.1.call-start = ((), (), s32[]{:S(2)}) async-start(), calls=%async_computation.4 | async-start | bytes 1966080 | tf_op jit(solution)/shard_map/reduce_scatter | solution.py:97
  616.6 34.2 %copy-start.1 = (bf16[256,5120]{1,0:T(8,128)(2,1)S(1)}, bf16[256,5120]{1,0:T(8,128)(2,1)}, u32[]{:S(2)}) copy-start(bf16[256,5120]{1,0:T(8,128)(2,1)} %param.16) | copy-start | bytes 7864324
  616.6 31.9 %reduce-scatter.6.cloned.1.call-start = ((), (), s32[]{:S(2)}) async-start(), calls=%async_computation.5 | async-start | bytes 1966080 | tf_op jit(solution)/shard_map/reduce_scatter | solution.py:100
Sparse Core Ops, SparseCore 0:
  10.8 89.0 all-gather.2
  334.5 238.6 all-reduce.3
  606.0 11.6 reduce-scatter.7
  620.6 12.8 reduce-scatter.3
  635.7 12.8 reduce-scatter.5
where the time goes:
time: 661 us; the launch traced here: 658 us
  waiting for transfers between devices  260 us (39%)
  blocking collectives  165 us (25%)
  other arithmetic  96 us (15%)
  local copies, waits for them, and re-layouts  72.3 us (11%)
  matrix products  48.4 us (7%)
  between operations  14.9 us (2%)
    psum x1, waiting for transfers between devices, per_device(): mismatch = lax.psum(partial_sum, 'expert')  239 us
    unnamed x2, blocking collectives  165 us
    scatter-add x2, other arithmetic, per_device(): partial_sum.at[teacher_idx].add(teacher_part).at[student_idx]  61.7 us
    gather x1, local copies, waits for them, and re-layouts, per_device(): student_x = whole[student_idx]  18.7 us
    gather x1, local copies, waits for them, and re-layouts, per_device(): cotangent[student_idx]  18.5 us
    unnamed x20, local copies, waits for them, and re-layouts  15.7 us
    gather x1, local copies, waits for them, and re-layouts, per_device(): teacher_x = whole[teacher_idx]  14.1 us
  transfers between devices with their start and end apart: 5, of which 3 were waited for; matrix products, arithmetic and copies ran while one was open for 7% of the time, Pallas kernels for 0%

commit v1 on v0

v1 whole, which is shorter than its diff:
```python
import functools
import math

import jax
import jax.numpy as jnp
from jax import lax
from jax.experimental import pallas as pl
from jax.experimental.pallas import tpu as pltpu
from jax.sharding import PartitionSpec as P

F = 4096
E_ORIG = 4
META = 128
BF = jnp.bfloat16
F32 = jnp.float32
AXES = ("dp", "expert")
SIDE = 4


def coords(device):
    return device // 64, {"z": (device // 16) % SIDE, "y": (device // 4) % SIDE, "x": device % SIDE}


def number(core, at):
    return core * 64 + at["z"] * 16 + at["y"] * 4 + at["x"]


def swap_pairs(links):
    pairs = []
    for device in range(128):
        core, at = coords(device)
        axis, bits = links[core]
        pairs.append((device, number(core, {**at, axis: at[axis] ^ bits})))
    return pairs


def shift_pairs(axes, by):
    pairs = []
    for device in range(128):
        core, at = coords(device)
        axis = axes[core]
        pairs.append((device, number(core, {**at, axis: (at[axis] + by) % SIDE})))
    return pairs


def swap(value, links):
    return lax.ppermute(value, AXES, swap_pairs(links))


def shift(value, axes, by):
    return lax.ppermute(value, AXES, shift_pairs(axes, by))


FIRST = ("x", "z")
A3, A4 = (("y", 1), ("y", 3)), (("y", 3), ("y", 1))
B3, B4 = (("z", 1), ("x", 1)), (("z", 3), ("x", 3))
STEP5 = ((("z", 1), ("x", 1)), (("z", 3), ("x", 3)), (("y", 1), ("y", 3)))
STEP6 = ((("z", 3), ("x", 3)), (("z", 1), ("x", 1)), (("y", 3), ("y", 1)))


def join(*parts):
    return jnp.concatenate(parts, axis=0)


def grow(a32, b16):
    a64 = join(a32, swap(a32, A3))
    b32 = join(b16, swap(b16, B3))
    a64_far = swap(a64, A4)
    b64 = join(b32, swap(b32, B4))
    near = [join(v, swap(v, link)) for v, link in zip((a64, a64_far, b64), STEP5)]
    far = [swap(v, link) for v, link in zip(near, STEP6)]
    return near, far


def shrink(near, far):
    add = lambda mine, got: mine.astype(F32) + got.astype(F32)
    got = [swap(v, link) for v, link in zip(far, STEP6)]
    got = [(add(m[64:], g[64:]).astype(BF), add(m[:64], g[:64])) for m, g in zip(near, got)]
    a1, a2, b = [add(mine, swap(theirs, link)) for (theirs, mine), link in zip(got, STEP5)]
    a = add(a1, swap(a2.astype(BF), A4))
    b = add(b[:32], swap(b[32:].astype(BF), B4))
    a = add(a[:32], swap(a[32:].astype(BF), A3))
    b = add(b[:16], swap(b[16:].astype(BF), B3))
    return join(a, b)


def line_up_kernel(place_ref, own, one, two, three, a_ref, b_ref):
    place = place_ref[0]
    row = lax.broadcasted_iota(jnp.int32, (48, 64), 0)
    column = lax.broadcasted_iota(jnp.int32, (48, 64), 1)
    block, token = column // 16, column % 16
    source = (place + SIDE - block) % SIDE
    pick = jnp.where((row == source * 12 + token) & (token < 12), 1.0, 0.0).astype(BF)
    rows = jnp.concatenate([own[...], one[...], two[...], three[...]], axis=0)
    out = jnp.dot(pick, rows, preferred_element_type=F32).astype(BF)
    a_ref[...] = out[:32]
    b_ref[...] = out[32:]


def line_up(place, blocks):
    width = blocks[0].shape[1]
    vmem = pl.BlockSpec(memory_space=pltpu.VMEM)
    return pl.pallas_call(
        line_up_kernel,
        out_shape=[jax.ShapeDtypeStruct((32, width), BF), jax.ShapeDtypeStruct((16, width), BF)],
        in_specs=[pl.BlockSpec(memory_space=pltpu.SMEM)] + [vmem] * 4,
        out_specs=[vmem, vmem],
        compiler_params=pltpu.CompilerParams(vmem_limit_bytes=32 << 20),
    )(place, *blocks)


def forward_kernel(count, steps, info, *refs):
    xs, metas = refs[:count], refs[count : 2 * count]
    tg, tu, sg, su, h_ref, ab_ref, acc = refs[2 * count :]
    step = pl.program_id(0)
    x = jnp.concatenate([r[...] for r in xs], axis=0)
    w = jnp.concatenate([tg[...], tu[...], sg[...], su[...]], axis=1)
    part = jnp.dot(x, w, preferred_element_type=F32)

    @pl.when(step == 0)
    def _():
        acc[...] = part

    @pl.when(step > 0)
    def _():
        acc[...] += part

    @pl.when(step == steps - 1)
    def _():
        ids = jnp.concatenate([r[:, 1:2] for r in metas], axis=0).astype(F32)
        mask_t = ids == info[0].astype(F32)
        mask_s = jnp.zeros(ids.shape, F32)
        for i in range(E_ORIG):
            mask_s = mask_s + jnp.where(ids == float(i), info[1 + i].astype(F32), 0.0)
        mask_s = mask_s > 0.5
        gate, up = acc[:, 0:256], acc[:, 256:512]
        hid_t = gate * jax.nn.sigmoid(gate) * up
        h_ref[:, 128:384] = jnp.where(mask_t, -hid_t, 0.0).astype(BF)
        gate, up = acc[:, 512:640], acc[:, 640:768]
        sig = jax.nn.sigmoid(gate)
        silu = gate * sig
        h_ref[:, 0:128] = jnp.where(mask_s, silu * up, 0.0).astype(BF)
        ab_ref[:, 0:128] = jnp.where(mask_s, up * sig * (1.0 + gate * (1.0 - sig)), 0.0)
        ab_ref[:, 128:256] = jnp.where(mask_s, silu, 0.0)


def forward(info, chunks, tg, tu, sg, su):
    count, depth = len(chunks), tg.shape[0]
    rows, block = 128 * count, 512
    steps = depth // block
    at_k = lambda k: (k, 0)
    return pl.pallas_call(
        functools.partial(forward_kernel, count, steps),
        grid=(steps,),
        out_shape=[jax.ShapeDtypeStruct((rows, 384), BF), jax.ShapeDtypeStruct((rows, 256), F32)],
        in_specs=[pl.BlockSpec(memory_space=pltpu.SMEM)]
        + [pl.BlockSpec((128, block), lambda k: (0, k))] * count
        + [pl.BlockSpec((128, META), lambda k: (0, depth // META))] * count
        + [pl.BlockSpec((block, w.shape[1]), at_k) for w in (tg, tu, sg, su)],
        out_specs=[pl.BlockSpec((rows, 384), lambda k: (0, 0)), pl.BlockSpec((rows, 256), lambda k: (0, 0))],
        scratch_shapes=[pltpu.VMEM((rows, 768), F32)],
        compiler_params=pltpu.CompilerParams(vmem_limit_bytes=40 << 20),
        cost_estimate=pl.CostEstimate(flops=2 * rows * depth * 768, bytes_accessed=2 * depth * (rows + 768), transcendentals=0),
    )(info, *chunks, *chunks, tg, tu, sg, su)


def down_kernel(count, h_ref, sd, td, *outs):
    w = jnp.concatenate([sd[...], td[...]], axis=0)
    out = jnp.dot(h_ref[...], w, preferred_element_type=F32).astype(BF)
    for i in range(count):
        outs[i][...] = out[128 * i : 128 * (i + 1)]


def down(hidden, sd, td):
    rows, width = hidden.shape[0], sd.shape[1]
    count, block = rows // 128, 1280
    return pl.pallas_call(
        functools.partial(down_kernel, count),
        grid=(width // block,),
        out_shape=[jax.ShapeDtypeStruct((128, width), BF)] * count,
        in_specs=[
            pl.BlockSpec((rows, 384), lambda n: (0, 0)),
            pl.BlockSpec((128, block), lambda n: (0, n)),
            pl.BlockSpec((256, block), lambda n: (0, n)),
        ],
        out_specs=[pl.BlockSpec((128, block), lambda n: (0, n))] * count,
        compiler_params=pltpu.CompilerParams(vmem_limit_bytes=40 << 20),
        cost_estimate=pl.CostEstimate(flops=2 * rows * width * 384, bytes_accessed=2 * width * (rows + 384), transcendentals=0),
    )(hidden, sd, td)


def backward_kernel(count, half, core, *refs):
    xs, cs = refs[:count], refs[count : 2 * count]
    sd, h1, h2, ab1, ab2, send, keep, acc, gt, ht = refs[2 * count :]
    step = pl.program_id(0)
    c = jnp.concatenate([r[...] for r in cs], axis=0)

    @pl.when(step < 2 * half)
    def _():
        part = lax.dot_general(c, sd[...], (((1,), (1,)), ((), ())), preferred_element_type=F32)

        @pl.when(step == 0)
        def _():
            acc[...] = part

        @pl.when(step > 0)
        def _():
            acc[...] += part

    @pl.when(step == 2 * half - 1)
    def _():
        ab = jnp.concatenate([ab1[...], ab2[...]], axis=0)
        gt[0:128, :] = (acc[...] * ab[:, 0:128]).T.astype(BF)
        gt[128:256, :] = (acc[...] * ab[:, 128:256]).T.astype(BF)
        ht[...] = jnp.concatenate([h1[...], h2[...]], axis=0).astype(F32).T.astype(BF)

    @pl.when(step >= 2 * half)
    def _():
        x = jnp.concatenate([r[...] for r in xs], axis=0)
        out = jnp.concatenate(
            [jnp.dot(gt[...], x, preferred_element_type=F32), jnp.dot(ht[...], c, preferred_element_type=F32)],
            axis=0,
        )

        @pl.when(step < 3 * half)
        def _():
            send[...] = out.astype(BF)

        @pl.when(step >= 3 * half)
        def _():
            keep[...] = out


def backward(core, xs, cs, sd, h1, h2, ab1, ab2):
    count, width = len(xs), sd.shape[1]
    rows, block = 128 * count, 1280
    half = width // block // 2
    turn = lambda s, core: lax.rem(s + (1 - core[0]) * half, 2 * half)
    x_at = lambda s, core: (0, turn(jnp.maximum(s, 2 * half), core))
    c_at = lambda s, core: (0, turn(s, core))
    d_at = lambda s, core: (0, turn(jnp.minimum(s, 2 * half - 1), core))
    whole = lambda s, core: (0, 0)
    return pl.pallas_call(
        functools.partial(backward_kernel, count, half),
        grid_spec=pltpu.PrefetchScalarGridSpec(
            num_scalar_prefetch=1,
            grid=(4 * half,),
            in_specs=[pl.BlockSpec((128, block), x_at)] * count
            + [pl.BlockSpec((128, block), c_at)] * count
            + [pl.BlockSpec((128, block), d_at)]
            + [pl.BlockSpec((rows // 2, 128), whole)] * 2
            + [pl.BlockSpec((rows // 2, 256), whole)] * 2,
            out_specs=[
                pl.BlockSpec((384, block), lambda s, core: (0, jnp.clip(s - 2 * half, 0, half - 1))),
                pl.BlockSpec((384, block), lambda s, core: (0, jnp.maximum(s - 3 * half, 0))),
            ],
            scratch_shapes=[pltpu.VMEM((rows, 128), F32), pltpu.VMEM((256, rows), BF), pltpu.VMEM((128, rows), BF)],
        ),
        out_shape=[jax.ShapeDtypeStruct((384, width // 2), BF), jax.ShapeDtypeStruct((384, width // 2), F32)],
        compiler_params=pltpu.CompilerParams(vmem_limit_bytes=48 << 20),
        cost_estimate=pl.CostEstimate(flops=2 * rows * width * 512, bytes_accessed=6 * rows * width, transcendentals=0),
    )(core, *xs, *cs, sd, h1, h2, ab1, ab2)


def finish_kernel(keep, got, gate, up, low):
    out = keep[...] + got[...].astype(F32)
    gate[...] = out[0:128].T
    up[...] = out[128:256].T
    low[...] = out[256:384]


def finish(keep, got):
    width, block = keep.shape[1], 512
    wide = pl.BlockSpec((384, block), lambda n: (0, n))
    tall = pl.BlockSpec((block, 128), lambda n: (n, 0))
    return pl.pallas_call(
        finish_kernel,
        grid=(width // block,),
        out_shape=[jax.ShapeDtypeStruct((width, 128), F32)] * 2 + [jax.ShapeDtypeStruct((128, width), F32)],
        in_specs=[wide, wide],
        out_specs=[tall, tall, pl.BlockSpec((128, block), lambda n: (0, n))],
        compiler_params=pltpu.CompilerParams(vmem_limit_bytes=32 << 20),
    )(keep, got)


def per_device(
    tokens,
    router_weight,
    initial_id,
    group_map,
    teacher_gate,
    teacher_up,
    teacher_down,
    student_gate,
    student_up,
    student_down,
):
    core, owner = lax.axis_index("dp"), lax.axis_index("expert")
    total = tokens.shape[0] * 128
    place = jnp.where(core == 0, owner % SIDE, owner // 16).astype(jnp.int32).reshape(1)
    teacher_expert = owner * teacher_gate.shape[1] // F
    student_expert = owner * student_gate.shape[1] // F
    info = jnp.concatenate([teacher_expert.astype(jnp.int32).reshape(1), (group_map == student_expert).astype(jnp.int32)])

    meta = jnp.concatenate([router_weight[:, None], initial_id.astype(BF), jnp.zeros((12, META - 2), BF)], axis=1)
    own = jnp.pad(jnp.concatenate([tokens, meta], axis=1), ((0, 4), (0, 0)))
    a32, b16 = line_up(place, [own] + [shift(own, FIRST, by) for by in (1, 2, 3)])
    near, far = grow(a32, b16)

    weights = (teacher_gate, teacher_up, student_gate, student_up)
    h_near, ab_near = forward(info, near, *weights)
    h_far, ab_far = forward(info, far, *weights)
    far_out = down(h_far, student_down, teacher_down)
    near_out = down(h_near, student_down, teacher_down)

    rows48 = shrink(near_out, far_out)
    part = rows48.astype(BF)
    for by in (1, 2, 3):
        rows48 = rows48 + shift(part, FIRST, by).astype(F32)
    depth = tokens.shape[1]
    weight = join(a32[:, depth : depth + 1], b16[:, depth : depth + 1]).astype(F32)
    cotangent = (weight * (weight * rows48) * (1.0 / math.sqrt(total))).astype(BF)
    c_near, c_far = grow(cotangent[:32], cotangent[32:])

    send, keep = backward(
        core.astype(jnp.int32).reshape(1), near + far, c_near + c_far, student_down, h_near, h_far, ab_near, ab_far
    )
    got = lax.ppermute(send, "dp", [(0, 1), (1, 0)])
    return tuple(finish(keep, got))


def solution(mesh):
    placed = (
        P(("dp", "expert"), None),
        P(("dp", "expert")),
        P(("dp", "expert"), None),
        P(),
        P(None, "expert"),
        P(None, "expert"),
        P("expert", None),
        P(None, "expert"),
        P(None, "expert"),
        P("expert", None),
    )
    return jax.shard_map(
        per_device,
        mesh=mesh,
        in_specs=placed,
        out_specs=(P("dp", "expert"), P("dp", "expert"), P("expert", "dp")),
        check_vma=False,
    )
```

time: 661 us -> 281 us (0.43)
  blocking collectives: 165 us -> 0 us
  waiting for transfers between devices: 260 us -> 167 us
  other arithmetic: 96 us -> 5.13 us
  local copies, waits for them, and re-layouts: 72.3 us -> 18 us
  matrix products: 48.4 us -> 0 us
  starting transfers between devices: 0.45 us -> 44.8 us
  Pallas kernels: 0 us -> 44.1 us
  between operations: 14.9 us -> 1.04 us
    psum x1 -> x0, waiting for transfers between devices: 239 us -> none  [per_device(): mismatch = lax.psum(partial_sum, 'expert')]
    ppermute x0 -> x37, waiting for transfers between devices: none -> 167 us  [the longest x30 143 us: swap(): return lax.ppermute(value, AXES, swap_pairs(links))]
    unnamed x2 -> x0, blocking collectives: 165 us -> none
    scatter-add x2 -> x0, other arithmetic: 61.7 us -> none  [per_device(): partial_sum.at[teacher_idx].add(teacher_part).at[student_idx]]
    gather x5 -> x0, local copies, waits for them, and re-layouts: 56 us -> none  [the longest x1 18.7 us: per_device(): student_x = whole[student_idx]]
    dot_general x9 -> x0, matrix products: 48.4 us -> none  [the longest x1 9.01 us: per_device(): jnp.dot(teacher_hidden, teacher_down, preferred_element_type=jnp.float32)]
    ppermute x0 -> x37, starting transfers between devices: none -> 44.8 us  [the longest x30 20.4 us: swap(): return lax.ppermute(value, AXES, swap_pairs(links))]
    pallas_call x0 -> x7, Pallas kernels: none -> 44.1 us  [the longest x2 18.6 us: forward(): pl.pallas_call(functools.partial(forward_kernel, count, steps), grid=(ste...]
  transfers between devices with their start and end apart: 5 -> 37, of which waited for: 3 -> 31; matrix products, arithmetic and copies ran while one was open for 7% -> 3% of each run, Pallas kernels for 0% -> 4%
where the time goes in v1:
time: 281 us; the launch traced here: 280 us
  waiting for transfers between devices  167 us (59%)
  starting transfers between devices  44.8 us (16%)
  Pallas kernels  44.1 us (16%)
  local copies, waits for them, and re-layouts  18 us (6%)
  other arithmetic  5.13 us (2%)
    ppermute x30, waiting for transfers between devices, swap(): return lax.ppermute(value, AXES, swap_pairs(links))  143 us
    ppermute x30, starting transfers between devices, swap(): return lax.ppermute(value, AXES, swap_pairs(links))  20.4 us
    ppermute x6, waiting for transfers between devices, shift(): return lax.ppermute(value, AXES, shift_pairs(axes, by))  20.3 us
    pallas_call x2, Pallas kernels, forward(): pl.pallas_call(functools.partial(forward_kernel, count, steps), grid=(ste...  18.6 us
    ppermute x1, starting transfers between devices, per_device(): got = lax.ppermute(send, 'dp', [(0, 1), (1, 0)])  17.1 us
    pallas_call x1, Pallas kernels, backward(): pl.pallas_call(functools.partial(backward_kernel, count, half), grid_spec...  14.8 us
    unnamed x46, local copies, waits for them, and re-layouts  14.6 us
    ppermute x6, starting transfers between devices, shift(): return lax.ppermute(value, AXES, shift_pairs(axes, by))  7.33 us
  transfers between devices with their start and end apart: 37, of which 31 were waited for; matrix products, arithmetic and copies ran while one was open for 3% of the time, Pallas kernels for 4%

profile of v1, /device:TPU:1, one launch (start us, length us, event | category | flops | bytes accessed | tf_op | source)
XLA Modules:
  0.0 279.9 jit_solution(1550354598986518075)
XLA Ops:
  3.2 4.7 %collective-permute-start.2 = (bf16[16,5248]{1,0:T(8,128)(2,1)S(1)}, bf16[16,5248]{1,0:T(8,128)(2,1)S(1)}, u32[]{:S(2)}, u32[]{:S(2)}) collective-permute-start(bf16[16,5248]{1,0:T(8,128)(2,1)S(1)} %pad.4.own), channel_id=1, source_target_pairs={{0,3},{1,0},{2,1},{3,2},{4,7},{5,4},{6,5},{7,6},{8,11},{9,8},{10,9... | collective-permute-start | bytes 503816 | tf_op jit(solution)/shard_map/ppermute | solution.py:51
  26.1 4.7 %collective-permute-done.8 = bf16[32,5248]{1,0:T(8,128)(2,1)S(1)} collective-permute-done((bf16[32,5248]{1,0:T(8,128)(2,1)S(1)}, bf16[32,5248]{1,0:T(8,128)(2,1)S(1)}, u32[]{:S(2)}, u32[]{:S(2)}) %collective-permute-start.8) | collective-permute-done | bytes 335904 | tf_op jit(solution)/shard_map/ppermute | solution.py:47
  31.6 4.3 %collective-permute-done.4 = bf16[64,5248]{1,0:T(8,128)(2,1)S(1)} collective-permute-done((bf16[64,5248]{1,0:T(8,128)(2,1)S(1)}, bf16[64,5248]{1,0:T(8,128)(2,1)S(1)}, u32[]{:S(2)}, u32[]{:S(2)}) %collective-permute-start.4) | collective-permute-done | bytes 671776 | tf_op jit(solution)/shard_map/ppermute | solution.py:47
  38.8 8.6 %collective-permute-done.9 = bf16[64,5248]{1,0:T(8,128)(2,1)S(1)} collective-permute-done((bf16[64,5248]{1,0:T(8,128)(2,1)S(1)}, bf16[64,5248]{1,0:T(8,128)(2,1)S(1)}, u32[]{:S(2)}, u32[]{:S(2)}) %collective-permute-start.9) | collective-permute-done | bytes 671776 | tf_op jit(solution)/shard_map/ppermute | solution.py:47
  48.4 13.4 %collective-permute-done.6 = bf16[64,5248]{1,0:T(8,128)(2,1)S(1)} collective-permute-done((bf16[64,5248]{1,0:T(8,128)(2,1)S(1)}, bf16[64,5248]{1,0:T(8,128)(2,1)S(1)}, u32[]{:S(2)}, u32[]{:S(2)}) %collective-permute-start.6) | collective-permute-done | bytes 671776 | tf_op jit(solution)/shard_map/ppermute | solution.py:47
  62.0 3.8 %collective-permute-done.12.refs_2_.refs_5_ = bf16[128,5248]{1,0:T(8,128)(2,1)} collective-permute-done((bf16[128,5248]{1,0:T(8,128)(2,1)}, bf16[128,5248]{1,0:T(8,128)(2,1)}, u32[]{:S(2)}, u32[]{:S(2)}) %collective-permute-start.12) | collective-permute-done | bytes 1343520 | tf_op jit(solution)/shard_map/ppermute | solution.py:47
  65.8 13.3 %collective-permute-done.11.refs_1_.refs_4_ = bf16[128,5248]{1,0:T(8,128)(2,1)} collective-permute-done((bf16[128,5248]{1,0:T(8,128)(2,1)S(1)}, bf16[128,5248]{1,0:T(8,128)(2,1)}, u32[]{:S(2)}, u32[]{:S(2)}) %collective-permute-start.11) | collective-permute-done | bytes 1343520 | tf_op jit(solution)/shard_map/ppermute | solution.py:47
  85.2 9.4 %shard_map.124 = (bf16[384,384]{1,0:T(8,128)(2,1)S(1)}, f32[384,256]{1,0:T(8,128)S(1)}) custom-call(s32[5]{0:T(128)S(1)} %pad_add_fusion.info, bf16[128,5248]{1,0:T(8,128)(2,1)} %collective-permute-done.10.refs_0_.refs_3_, bf16[128,5248]{1,0:T(8,128)(2,1)} %collective-permute-done.11.refs_1_.refs_4_, ...), custom_call_target="tpu_custom_call" | custom-call | flops 3019898880 | bytes 11796480 | tf_op jit(solution)/shard_map/pallas_call | solution.py:152
  97.7 3.9 %shard_map.125 = (bf16[128,5120]{1,0:T(8,128)(2,1)S(1)}, bf16[128,5120]{1,0:T(8,128)(2,1)}, bf16[128,5120]{1,0:T(8,128)(2,1)}) custom-call(bf16[384,384]{1,0:T(8,128)(2,1)S(1)} %get-tuple-element.21.h_ref.refs_14_, bf16[128,5120]{1,0:T(8,128)(2,1)S(1)} %copy-done.11, bf16[256,5120]{1,0:T(8,128)(2,1)S(1)} %copy-done.13), custom_call_target="tpu_custom_call" | custom-call | flops 1509949440 | bytes 7864320 | tf_op jit(solution)/shard_map/pallas_call | solution.py:177
  103.0 9.1 %shard_map.122 = (bf16[384,384]{1,0:T(8,128)(2,1)S(1)}, f32[384,256]{1,0:T(8,128)S(1)}) custom-call(s32[5]{0:T(128)S(1)} %pad_add_fusion.info, bf16[128,5248]{1,0:T(8,128)(2,1)S(1)} %constant_dynamic-update-slice_fusion.2.refs_0_.refs_3_, bf16[128,5248]{1,0:T(8,128)(2,1)S(1)} %constant_dynamic-update-slice_fusion.5.refs_1_.refs_4_, ...), custom_call_target="tpu_custom_call" | custom-call | flops 3019898880 | bytes 11796480 | tf_op jit(solution)/shard_map/pallas_call | solution.py:152
  120.9 8.4 %collective-permute-done.15 = bf16[128,5120]{1,0:T(8,128)(2,1)S(1)} collective-permute-done((bf16[128,5120]{1,0:T(8,128)(2,1)}, bf16[128,5120]{1,0:T(8,128)(2,1)S(1)}, u32[]{:S(2)}, u32[]{:S(2)}) %collective-permute-start.15) | collective-permute-done | bytes 1310752 | tf_op jit(solution)/shard_map/ppermute | solution.py:47
  136.2 4.3 %collective-permute-done.16 = bf16[64,5120]{1,0:T(8,128)(2,1)S(1)} collective-permute-done((bf16[64,5120]{1,0:T(8,128)(2,1)S(1)}, bf16[64,5120]{1,0:T(8,128)(2,1)S(1)}, u32[]{:S(2)}, u32[]{:S(2)}) %collective-permute-start.16) | collective-permute-done | bytes 655392 | tf_op jit(solution)/shard_map/ppermute | solution.py:47
  144.6 6.0 %collective-permute-done.17 = bf16[64,5120]{1,0:T(8,128)(2,1)S(1)} collective-permute-done((bf16[64,5120]{1,0:T(8,128)(2,1)S(1)}, bf16[64,5120]{1,0:T(8,128)(2,1)S(1)}, u32[]{:S(2)}, u32[]{:S(2)}) %collective-permute-start.17) | collective-permute-done | bytes 655392 | tf_op jit(solution)/shard_map/ppermute | solution.py:47
  151.4 10.6 %collective-permute-done.18 = bf16[32,5120]{1,0:T(8,128)(2,1)S(1)} collective-permute-done((bf16[32,5120]{1,0:T(8,128)(2,1)S(1)}, bf16[32,5120]{1,0:T(8,128)(2,1)S(1)}, u32[]{:S(2)}, u32[]{:S(2)}) %collective-permute-start.18) | collective-permute-done | bytes 327712 | tf_op jit(solution)/shard_map/ppermute | solution.py:47
  164.4 5.8 %collective-permute-done.25 = bf16[48,5120]{1,0:T(8,128)(2,1)S(1)} collective-permute-done((bf16[48,5120]{1,0:T(8,128)(2,1)S(1)}, bf16[48,5120]{1,0:T(8,128)(2,1)S(1)}, u32[]{:S(2)}, u32[]{:S(2)}) %collective-permute-start.25) | collective-permute-done | bytes 491552 | tf_op jit(solution)/shard_map/ppermute | solution.py:51
  172.7 5.2 %collective-permute-done.23 = bf16[48,5120]{1,0:T(8,128)(2,1)S(1)} collective-permute-done((bf16[48,5120]{1,0:T(8,128)(2,1)S(1)}, bf16[48,5120]{1,0:T(8,128)(2,1)S(1)}, u32[]{:S(2)}, u32[]{:S(2)}) %collective-permute-start.23) | collective-permute-done | bytes 491552 | tf_op jit(solution)/shard_map/ppermute | solution.py:51
  178.5 6.1 %collective-permute-done.30 = bf16[16,5120]{1,0:T(8,128)(2,1)S(1)} collective-permute-done((bf16[16,5120]{1,0:T(8,128)(2,1)S(1)}, bf16[16,5120]{1,0:T(8,128)(2,1)S(1)}, u32[]{:S(2)}, u32[]{:S(2)}) %collective-permute-start.30) | collective-permute-done | bytes 163872 | tf_op jit(solution)/shard_map/ppermute | solution.py:47
  187.3 4.5 %collective-permute-done.31 = bf16[32,5120]{1,0:T(8,128)(2,1)S(1)} collective-permute-done((bf16[32,5120]{1,0:T(8,128)(2,1)S(1)}, bf16[32,5120]{1,0:T(8,128)(2,1)S(1)}, u32[]{:S(2)}, u32[]{:S(2)}) %collective-permute-start.31) | collective-permute-done | bytes 327712 | tf_op jit(solution)/shard_map/ppermute | solution.py:47
  202.8 18.1 %collective-permute-done.29 = bf16[64,5120]{1,0:T(8,128)(2,1)S(1)} collective-permute-done((bf16[64,5120]{1,0:T(8,128)(2,1)S(1)}, bf16[64,5120]{1,0:T(8,128)(2,1)S(1)}, u32[]{:S(2)}, u32[]{:S(2)}) %collective-permute-start.29) | collective-permute-done | bytes 655392 | tf_op jit(solution)/shard_map/ppermute | solution.py:47
  221.1 5.5 %collective-permute-done.35.refs_11_ = bf16[128,5120]{1,0:T(8,128)(2,1)S(1)} collective-permute-done((bf16[128,5120]{1,0:T(8,128)(2,1)S(1)}, bf16[128,5120]{1,0:T(8,128)(2,1)S(1)}, u32[]{:S(2)}, u32[]{:S(2)}) %collective-permute-start.35) | collective-permute-done | bytes 1310752 | tf_op jit(solution)/shard_map/ppermute | solution.py:47
  226.6 11.2 %collective-permute-done.34.refs_10_ = bf16[128,5120]{1,0:T(8,128)(2,1)S(1)} collective-permute-done((bf16[128,5120]{1,0:T(8,128)(2,1)S(1)}, bf16[128,5120]{1,0:T(8,128)(2,1)S(1)}, u32[]{:S(2)}, u32[]{:S(2)}) %collective-permute-start.34) | collective-permute-done | bytes 1310752 | tf_op jit(solution)/shard_map/ppermute | solution.py:47
  238.8 14.8 %shard_map.126 = (bf16[384,2560]{1,0:T(8,128)(2,1)}, f32[384,2560]{1,0:T(8,128)}) custom-call(s32[1]{0:T(128)} %bitcast.core, bf16[128,5248]{1,0:T(8,128)(2,1)} %copy-done.1, bf16[128,5248]{1,0:T(8,128)(2,1)} %copy-done, bf16[128,5248]{1,0:T(8,128)(2,1)} %constant_dynamic-update-slice_fusion.7.refs_2_.refs_5_, ...), custom_call_target="tpu_custom_call" | custom-call | flops 4026531840 | bytes 23592960 | tf_op jit(solution)/shard_map/pallas_call | solution.py:243
  253.6 17.1 %collective-permute-start.36 = (bf16[384,2560]{1,0:T(8,128)(2,1)}, bf16[384,2560]{1,0:T(8,128)(2,1)S(1)}, u32[]{:S(2)}, u32[]{:S(2)}) collective-permute-start(bf16[384,2560]{1,0:T(8,128)(2,1)} %get-tuple-element.30), channel_id=1, source_target_pairs={{0,64},{64,0},{1,65},{65,1},{2,66},{66,2},{3,67},{67,3},{4,68},{68... | collective-permute-start | bytes 5898248 | tf_op jit(solution)/shard_map/ppermute | solution.py:328
  270.7 3.8 %collective-permute-done.36.got = bf16[384,2560]{1,0:T(8,128)(2,1)S(1)} collective-permute-done((bf16[384,2560]{1,0:T(8,128)(2,1)}, bf16[384,2560]{1,0:T(8,128)(2,1)S(1)}, u32[]{:S(2)}, u32[]{:S(2)}) %collective-permute-start.36) | collective-permute-done | bytes 1966112 | tf_op jit(solution)/shard_map/ppermute | solution.py:328
  (142 shorter events, 82.4 us)
Async XLA Ops:
  15.7 10.1 %collective-permute-start.3 = (bf16[32,5248]{1,0:T(8,128)(2,1)S(1)}, bf16[32,5248]{1,0:T(8,128)(2,1)S(1)}, u32[]{:S(2)}, u32[]{:S(2)}) collective-permute-start(bf16[32,5248]{1,0:T(8,128)(2,1)S(1)} %get-tuple-element.17), channel_id=1, source_target_pairs={{0,4},{1,5},{2,6},{3,7},{4,0},{5,1},{6,2},{7,3},{8,12},{9,13},{10,... | collective-permute-start | bytes 1007624 | tf_op jit(solution)/shard_map/ppermute | solution.py:47
  25.9 11.0 %collective-permute-start.5 = (bf16[64,5248]{1,0:T(8,128)(2,1)S(1)}, bf16[64,5248]{1,0:T(8,128)(2,1)S(1)}, u32[]{:S(2)}, u32[]{:S(2)}) collective-permute-start(bf16[64,5248]{1,0:T(8,128)(2,1)S(1)} %get-tuple-element.31), channel_id=1, source_target_pairs={{0,12},{1,13},{2,14},{3,15},{4,8},{5,9},{6,10},{7,11},{8,4},{9,5},... | collective-permute-start | bytes 2015240 | tf_op jit(solution)/shard_map/ppermute | solution.py:47
  26.0 10.0 %collective-permute-start.4 = (bf16[64,5248]{1,0:T(8,128)(2,1)S(1)}, bf16[64,5248]{1,0:T(8,128)(2,1)S(1)}, u32[]{:S(2)}, u32[]{:S(2)}) collective-permute-start(bf16[64,5248]{1,0:T(8,128)(2,1)S(1)} %get-tuple-element.31), channel_id=1, source_target_pairs={{0,16},{1,17},{2,18},{3,19},{4,20},{5,21},{6,22},{7,23},{8,24},{9,... | collective-permute-start | bytes 2015240 | tf_op jit(solution)/shard_map/ppermute | solution.py:47
  30.8 16.7 %collective-permute-start.9 = (bf16[64,5248]{1,0:T(8,128)(2,1)S(1)}, bf16[64,5248]{1,0:T(8,128)(2,1)S(1)}, u32[]{:S(2)}, u32[]{:S(2)}) collective-permute-start(bf16[64,5248]{1,0:T(8,128)(2,1)S(1)} %pad_maximum_fusion.3), channel_id=1, source_target_pairs={{0,4},{1,5},{2,6},{3,7},{4,0},{5,1},{6,2},{7,3},{8,12},{9,13},{10,... | collective-permute-start | bytes 2015240 | tf_op jit(solution)/shard_map/ppermute | solution.py:47
  36.0 26.0 %collective-permute-start.10 = (bf16[128,5248]{1,0:T(8,128)(2,1)S(1)}, bf16[128,5248]{1,0:T(8,128)(2,1)}, u32[]{:S(2)}, u32[]{:S(2)}) collective-permute-start(bf16[128,5248]{1,0:T(8,128)(2,1)S(1)} %constant_dynamic-update-slice_fusion.2.refs_0_.refs_3_), channel_id=1, source_target_pairs={{0,48},{1,49},{2,50},{3,51},{4,52},{5,53},{6,54},{7,55},{8,56},{9,... | collective-permute-start | bytes 4030472 | tf_op jit(solution)/shard_map/ppermute | solution.py:47
  36.9 24.8 %collective-permute-start.6 = (bf16[64,5248]{1,0:T(8,128)(2,1)S(1)}, bf16[64,5248]{1,0:T(8,128)(2,1)S(1)}, u32[]{:S(2)}, u32[]{:S(2)}) collective-permute-start(bf16[64,5248]{1,0:T(8,128)(2,1)S(1)} %collective-permute-done.5), channel_id=1, source_target_pairs={{0,48},{1,49},{2,50},{3,51},{4,52},{5,53},{6,54},{7,55},{8,56},{9,... | collective-permute-start | bytes 2015240 | tf_op jit(solution)/shard_map/ppermute | solution.py:47
  48.4 17.4 %collective-permute-start.12 = (bf16[128,5248]{1,0:T(8,128)(2,1)}, bf16[128,5248]{1,0:T(8,128)(2,1)}, u32[]{:S(2)}, u32[]{:S(2)}) collective-permute-start(bf16[128,5248]{1,0:T(8,128)(2,1)} %constant_dynamic-update-slice_fusion.7.refs_2_.refs_5_), channel_id=1, source_target_pairs={{0,12},{1,13},{2,14},{3,15},{4,8},{5,9},{6,10},{7,11},{8,4},{9,5},... | collective-permute-start | bytes 4030472 | tf_op jit(solution)/shard_map/ppermute | solution.py:47
  61.8 17.3 %collective-permute-start.11 = (bf16[128,5248]{1,0:T(8,128)(2,1)S(1)}, bf16[128,5248]{1,0:T(8,128)(2,1)}, u32[]{:S(2)}, u32[]{:S(2)}) collective-permute-start(bf16[128,5248]{1,0:T(8,128)(2,1)S(1)} %constant_dynamic-update-slice_fusion.5.refs_1_.refs_4_), channel_id=1, source_target_pairs={{0,16},{1,17},{2,18},{3,19},{4,20},{5,21},{6,22},{7,23},{8,24},{9,... | collective-permute-start | bytes 4030472 | tf_op jit(solution)/shard_map/ppermute | solution.py:47
  101.7 17.1 %collective-permute-start.19 = (bf16[128,5120]{1,0:T(8,128)(2,1)}, bf16[128,5120]{1,0:T(8,128)(2,1)}, u32[]{:S(2)}, u32[]{:S(2)}) collective-permute-start(bf16[128,5120]{1,0:T(8,128)(2,1)} %get-tuple-element.26), channel_id=1, source_target_pairs={{0,12},{1,13},{2,14},{3,15},{4,8},{5,9},{6,10},{7,11},{8,4},{9,5},... | collective-permute-start | bytes 3932168 | tf_op jit(solution)/shard_map/ppermute | solution.py:47
  112.1 17.1 %collective-permute-start.15 = (bf16[128,5120]{1,0:T(8,128)(2,1)}, bf16[128,5120]{1,0:T(8,128)(2,1)S(1)}, u32[]{:S(2)}, u32[]{:S(2)}) collective-permute-start(bf16[128,5120]{1,0:T(8,128)(2,1)} %get-tuple-element.24), channel_id=1, source_target_pairs={{0,16},{1,17},{2,18},{3,19},{4,20},{5,21},{6,22},{7,23},{8,24},{9,... | collective-permute-start | bytes 3932168 | tf_op jit(solution)/shard_map/ppermute | solution.py:47
  115.5 18.0 %collective-permute-start.13 = (bf16[128,5120]{1,0:T(8,128)(2,1)S(1)}, bf16[128,5120]{1,0:T(8,128)(2,1)S(1)}, u32[]{:S(2)}, u32[]{:S(2)}) collective-permute-start(bf16[128,5120]{1,0:T(8,128)(2,1)S(1)} %copy-done.15), channel_id=1, source_target_pairs={{0,48},{1,49},{2,50},{3,51},{4,52},{5,53},{6,54},{7,55},{8,56},{9,... | collective-permute-start | bytes 3932168 | tf_op jit(solution)/shard_map/ppermute | solution.py:47
  120.0 14.5 %collective-permute-start.20 = (bf16[64,5120]{1,0:T(8,128)(2,1)S(1)}, bf16[64,5120]{1,0:T(8,128)(2,1)S(1)}, u32[]{:S(2)}, u32[]{:S(2)}) collective-permute-start(bf16[64,5120]{1,0:T(8,128)(2,1)S(1)} %add_convert_fusion), channel_id=1, source_target_pairs={{0,4},{1,5},{2,6},{3,7},{4,0},{5,1},{6,2},{7,3},{8,12},{9,13},{10,... | collective-permute-start | bytes 1966088 | tf_op jit(solution)/shard_map/ppermute | solution.py:47
  129.4 11.1 %collective-permute-start.16 = (bf16[64,5120]{1,0:T(8,128)(2,1)S(1)}, bf16[64,5120]{1,0:T(8,128)(2,1)S(1)}, u32[]{:S(2)}, u32[]{:S(2)}) collective-permute-start(bf16[64,5120]{1,0:T(8,128)(2,1)S(1)} %add_convert_fusion.2), channel_id=1, source_target_pairs={{0,48},{1,49},{2,50},{3,51},{4,52},{5,53},{6,54},{7,55},{8,56},{9,... | collective-permute-start | bytes 1966088 | tf_op jit(solution)/shard_map/ppermute | solution.py:47
  133.7 10.9 %collective-permute-start.14 = (bf16[64,5120]{1,0:T(8,128)(2,1)S(1)}, bf16[64,5120]{1,0:T(8,128)(2,1)S(1)}, u32[]{:S(2)}, u32[]{:S(2)}) collective-permute-start(bf16[64,5120]{1,0:T(8,128)(2,1)S(1)} %add_convert_fusion.3), channel_id=1, source_target_pairs={{0,16},{1,17},{2,18},{3,19},{4,20},{5,21},{6,22},{7,23},{8,24},{9,... | collective-permute-start | bytes 1966088 | tf_op jit(solution)/shard_map/ppermute | solution.py:47
  150.9 11.0 %collective-permute-start.18 = (bf16[32,5120]{1,0:T(8,128)(2,1)S(1)}, bf16[32,5120]{1,0:T(8,128)(2,1)S(1)}, u32[]{:S(2)}, u32[]{:S(2)}) collective-permute-start(bf16[32,5120]{1,0:T(8,128)(2,1)S(1)} %slice.126), channel_id=1, source_target_pairs={{0,4},{1,5},{2,6},{3,7},{4,0},{5,1},{6,2},{7,3},{8,12},{9,13},{10,... | collective-permute-start | bytes 983048 | tf_op jit(solution)/shard_map/ppermute | solution.py:47
  163.4 14.5 %collective-permute-start.23 = (bf16[48,5120]{1,0:T(8,128)(2,1)S(1)}, bf16[48,5120]{1,0:T(8,128)(2,1)S(1)}, u32[]{:S(2)}, u32[]{:S(2)}) collective-permute-start(bf16[48,5120]{1,0:T(8,128)(2,1)S(1)} %fusion), channel_id=1, source_target_pairs={{0,1},{1,2},{2,3},{3,0},{4,5},{5,6},{6,7},{7,4},{8,9},{9,10},{10,1... | collective-permute-start | bytes 1474568 | tf_op jit(solution)/shard_map/ppermute | solution.py:51
  185.9 9.8 %collective-permute-start.27 = (bf16[64,5120]{1,0:T(8,128)(2,1)S(1)}, bf16[64,5120]{1,0:T(8,128)(2,1)S(1)}, u32[]{:S(2)}, u32[]{:S(2)}) collective-permute-start(bf16[64,5120]{1,0:T(8,128)(2,1)S(1)} %pad_maximum_fusion.4), channel_id=1, source_target_pairs={{0,16},{1,17},{2,18},{3,19},{4,20},{5,21},{6,22},{7,23},{8,24},{9,... | collective-permute-start | bytes 1966088 | tf_op jit(solution)/shard_map/ppermute | solution.py:47
  187.3 13.2 %collective-permute-start.28 = (bf16[64,5120]{1,0:T(8,128)(2,1)S(1)}, bf16[64,5120]{1,0:T(8,128)(2,1)S(1)}, u32[]{:S(2)}, u32[]{:S(2)}) collective-permute-start(bf16[64,5120]{1,0:T(8,128)(2,1)S(1)} %pad_maximum_fusion.4), channel_id=1, source_target_pairs={{0,12},{1,13},{2,14},{3,15},{4,8},{5,9},{6,10},{7,11},{8,4},{9,5},... | collective-permute-start | bytes 1966088 | tf_op jit(solution)/shard_map/ppermute | solution.py:47
  191.9 10.7 %collective-permute-start.32 = (bf16[64,5120]{1,0:T(8,128)(2,1)S(1)}, bf16[64,5120]{1,0:T(8,128)(2,1)S(1)}, u32[]{:S(2)}, u32[]{:S(2)}) collective-permute-start(bf16[64,5120]{1,0:T(8,128)(2,1)S(1)} %pad_maximum_fusion.5), channel_id=1, source_target_pairs={{0,4},{1,5},{2,6},{3,7},{4,0},{5,1},{6,2},{7,3},{8,12},{9,13},{10,... | collective-permute-start | bytes 1966088 | tf_op jit(solution)/shard_map/ppermute | solution.py:47
  195.8 25.3 %collective-permute-start.33 = (bf16[128,5120]{1,0:T(8,128)(2,1)S(1)}, bf16[128,5120]{1,0:T(8,128)(2,1)S(1)}, u32[]{:S(2)}, u32[]{:S(2)}) collective-permute-start(bf16[128,5120]{1,0:T(8,128)(2,1)S(1)} %pad_maximum_fusion.refs_6_), channel_id=1, source_target_pairs={{0,48},{1,49},{2,50},{3,51},{4,52},{5,53},{6,54},{7,55},{8,56},{9,... | collective-permute-start | bytes 3932168 | tf_op jit(solution)/shard_map/ppermute | solution.py:47
  200.5 20.4 %collective-permute-start.29 = (bf16[64,5120]{1,0:T(8,128)(2,1)S(1)}, bf16[64,5120]{1,0:T(8,128)(2,1)S(1)}, u32[]{:S(2)}, u32[]{:S(2)}) collective-permute-start(bf16[64,5120]{1,0:T(8,128)(2,1)S(1)} %collective-permute-done.28), channel_id=1, source_target_pairs={{0,48},{1,49},{2,50},{3,51},{4,52},{5,53},{6,54},{7,55},{8,56},{9,... | collective-permute-start | bytes 1966088 | tf_op jit(solution)/shard_map/ppermute | solution.py:47
  202.7 23.9 %collective-permute-start.35 = (bf16[128,5120]{1,0:T(8,128)(2,1)S(1)}, bf16[128,5120]{1,0:T(8,128)(2,1)S(1)}, u32[]{:S(2)}, u32[]{:S(2)}) collective-permute-start(bf16[128,5120]{1,0:T(8,128)(2,1)S(1)} %pad_maximum_fusion.1.refs_8_), channel_id=1, source_target_pairs={{0,12},{1,13},{2,14},{3,15},{4,8},{5,9},{6,10},{7,11},{8,4},{9,5},... | collective-permute-start | bytes 3932168 | tf_op jit(solution)/shard_map/ppermute | solution.py:47
  220.9 16.8 %collective-permute-start.34 = (bf16[128,5120]{1,0:T(8,128)(2,1)S(1)}, bf16[128,5120]{1,0:T(8,128)(2,1)S(1)}, u32[]{:S(2)}, u32[]{:S(2)}) collective-permute-start(bf16[128,5120]{1,0:T(8,128)(2,1)S(1)} %constant_dynamic-update-slice_fusion.11.refs_7_), channel_id=1, source_target_pairs={{0,16},{1,17},{2,18},{3,19},{4,20},{5,21},{6,22},{7,23},{8,24},{9,... | collective-permute-start | bytes 3932168 | tf_op jit(solution)/shard_map/ppermute | solution.py:47
  253.6 20.9 %collective-permute-start.36 = (bf16[384,2560]{1,0:T(8,128)(2,1)}, bf16[384,2560]{1,0:T(8,128)(2,1)S(1)}, u32[]{:S(2)}, u32[]{:S(2)}) collective-permute-start(bf16[384,2560]{1,0:T(8,128)(2,1)} %get-tuple-element.30), channel_id=1, source_target_pairs={{0,64},{64,0},{1,65},{65,1},{2,66},{66,2},{3,67},{67,3},{4,68},{68... | collective-permute-start | bytes 5898248 | tf_op jit(solution)/shard_map/ppermute | solution.py:328
  (33 other events, 339.6 us)

commit v2 on v1

--- a/solution.py
+++ b/solution.py
@@ -25,88 +25,99 @@
     return core * 64 + at["z"] * 16 + at["y"] * 4 + at["x"]
 
 
-def swap_pairs(links):
-    pairs = []
+def join(*parts):
+    return jnp.concatenate(parts, axis=0)
+
+
+ORDERS = (("x", "y", "z"), ("y", "z", "x"), ("z", "x", "y"))
+PIECES = range(3)
+CROSS = (3, 5)
+
+
+def step_pairs(piece, step):
+    axis, pairs = ORDERS[piece][step // 2], []
     for device in range(128):
         core, at = coords(device)
-        axis, bits = links[core]
-        pairs.append((device, number(core, {**at, axis: at[axis] ^ bits})))
+        bits = (1, 3)[(step + core) % 2]
+        pairs.append((device, number(core ^ (step in CROSS), {**at, axis: at[axis] ^ bits})))
     return pairs
 
 
-def shift_pairs(axes, by):
-    pairs = []
-    for device in range(128):
-        core, at = coords(device)
-        axis = axes[core]
-        pairs.append((device, number(core, {**at, axis: (at[axis] + by) % SIDE})))
-    return pairs
-
-
-def swap(value, links):
-    return lax.ppermute(value, AXES, swap_pairs(links))
-
-
-def shift(value, axes, by):
-    return lax.ppermute(value, AXES, shift_pairs(axes, by))
-
-
-FIRST = ("x", "z")
-A3, A4 = (("y", 1), ("y", 3)), (("y", 3), ("y", 1))
-B3, B4 = (("z", 1), ("x", 1)), (("z", 3), ("x", 3))
-STEP5 = ((("z", 1), ("x", 1)), (("z", 3), ("x", 3)), (("y", 1), ("y", 3)))
-STEP6 = ((("z", 3), ("x", 3)), (("z", 1), ("x", 1)), (("y", 3), ("y", 1)))
-
-
-def join(*parts):
-    return jnp.concatenate(parts, axis=0)
-
-
-def grow(a32, b16):
-    a64 = join(a32, swap(a32, A3))
-    b32 = join(b16, swap(b16, B3))
-    a64_far = swap(a64, A4)
-    b64 = join(b32, swap(b32, B4))
-    near = [join(v, swap(v, link)) for v, link in zip((a64, a64_far, b64), STEP5)]
-    far = [swap(v, link) for v, link in zip(near, STEP6)]
-    return near, far
+def hop(value, piece, step):
+    return lax.ppermute(value, AXES, step_pairs(piece, step))
+
+
+def hop_back(value, piece, step):
+    return lax.ppermute(value, AXES, [(to, own) for own, to in step_pairs(piece, step)])
+
+
+def together(values):
+    return lax.optimization_barrier(tuple(values))
+
+
+def grow(parts):
+    for step in (3, 4):
+        parts = [join(v, hop(v, p, step)) for p, v in enumerate(parts)]
+    return parts, [hop(v, p, 5) for p, v in enumerate(parts)]
+
+
+def add(mine, got):
+    return mine.astype(F32) + got.astype(F32)
 
 
 def shrink(near, far):
-    add = lambda mine, got: mine.astype(F32) + got.astype(F32)
-    got = [swap(v, link) for v, link in zip(far, STEP6)]
-    got = [(add(m[64:], g[64:]).astype(BF), add(m[:64], g[:64])) for m, g in zip(near, got)]
-    a1, a2, b = [add(mine, swap(theirs, link)) for (theirs, mine), link in zip(got, STEP5)]
-    a = add(a1, swap(a2.astype(BF), A4))
-    b = add(b[:32], swap(b[32:].astype(BF), B4))
-    a = add(a[:32], swap(a[32:].astype(BF), A3))
-    b = add(b[:16], swap(b[16:].astype(BF), B3))
-    return join(a, b)
-
-
-def line_up_kernel(place_ref, own, one, two, three, a_ref, b_ref):
-    place = place_ref[0]
-    row = lax.broadcasted_iota(jnp.int32, (48, 64), 0)
-    column = lax.broadcasted_iota(jnp.int32, (48, 64), 1)
-    block, token = column // 16, column % 16
-    source = (place + SIDE - block) % SIDE
-    pick = jnp.where((row == source * 12 + token) & (token < 12), 1.0, 0.0).astype(BF)
-    rows = jnp.concatenate([own[...], one[...], two[...], three[...]], axis=0)
-    out = jnp.dot(pick, rows, preferred_element_type=F32).astype(BF)
-    a_ref[...] = out[:32]
-    b_ref[...] = out[32:]
-
-
-def line_up(place, blocks):
-    width = blocks[0].shape[1]
+    sums = []
+    for p in PIECES:
+        mine, theirs = near[p], far[p]
+        for step in (5, 4, 3):
+            got = hop_back(theirs.astype(BF), p, step)
+            half = mine.shape[0] // 2
+            if step > 3:
+                theirs, mine = add(mine[half:], got[half:]), add(mine[:half], got[:half])
+            else:
+                mine = add(mine, got)
+        sums.append(mine)
+    for step in (2, 1, 0):
+        sums = [add(v, hop(v.astype(BF), p, step)) for p, v in enumerate(sums)]
+    return sums
+
+
+def line_up_kernel(place_ref, mine, got, out):
+    row = lax.broadcasted_iota(jnp.int32, (16, 32), 0)
+    column = lax.broadcasted_iota(jnp.int32, (16, 32), 1)
+    block, token = column // 8, column % 8
+    place = jnp.zeros((16, 32), jnp.int32)
+    for i in range(SIDE):
+        place = jnp.where(block == i, place_ref[i], place)
+    pick = jnp.where((row == place * 4 + token) & (token < 4), 1.0, 0.0).astype(BF)
+    rows = jnp.concatenate([mine[...], got[...]], axis=0)
+    out[...] = jnp.dot(pick, rows, preferred_element_type=F32).astype(BF)
+
+
+def line_up(places, mine, got):
     vmem = pl.BlockSpec(memory_space=pltpu.VMEM)
     return pl.pallas_call(
         line_up_kernel,
-        out_shape=[jax.ShapeDtypeStruct((32, width), BF), jax.ShapeDtypeStruct((16, width), BF)],
-        in_specs=[pl.BlockSpec(memory_space=pltpu.SMEM)] + [vmem] * 4,
-        out_specs=[vmem, vmem],
+        out_shape=jax.ShapeDtypeStruct((16, mine.shape[1]), BF),
+        in_specs=[pl.BlockSpec(memory_space=pltpu.SMEM), vmem, vmem],
+        out_specs=vmem,
         compiler_params=pltpu.CompilerParams(vmem_limit_bytes=32 << 20),
-    )(place, *blocks)
+    )(places, mine, got)
+
+
+def first_gather(own, core, at):
+    parts = []
+    for p in PIECES:
+        mine = jnp.pad(own[4 * p : 4 * p + 4], ((0, 4), (0, 0)))
+        mine = join(mine, hop(mine, p, 0))
+        got = hop(mine, p, 1)
+        flips = jnp.where(core == 0, jnp.array([0, 1, 3, 2]), jnp.array([0, 3, 1, 2])).astype(jnp.int32)
+        rows = line_up(at[ORDERS[p][0]] ^ flips, mine, got)
+        got = hop(rows, p, 2)
+        place = at[ORDERS[p][1]]
+        low = place < (place ^ jnp.where(core == 0, 1, 3))
+        parts.append(join(jnp.where(low, rows, got), jnp.where(low, got, rows)))
+    return parts
 
 
 def forward_kernel(count, steps, info, *refs):
@@ -146,7 +157,7 @@
 
 def forward(info, chunks, tg, tu, sg, su):
     count, depth = len(chunks), tg.shape[0]
-    rows, block = 128 * count, 512
+    rows, block = 128 * count, 1280
     steps = depth // block
     at_k = lambda k: (k, 0)
     return pl.pallas_call(
@@ -297,30 +308,28 @@
 ):
     core, owner = lax.axis_index("dp"), lax.axis_index("expert")
     total = tokens.shape[0] * 128
-    place = jnp.where(core == 0, owner % SIDE, owner // 16).astype(jnp.int32).reshape(1)
+    at = {"z": owner // 16, "y": (owner // SIDE) % SIDE, "x": owner % SIDE}
     teacher_expert = owner * teacher_gate.shape[1] // F
     student_expert = owner * student_gate.shape[1] // F
     info = jnp.concatenate([teacher_expert.astype(jnp.int32).reshape(1), (group_map == student_expert).astype(jnp.int32)])
 
     meta = jnp.concatenate([router_weight[:, None], initial_id.astype(BF), jnp.zeros((12, META - 2), BF)], axis=1)
-    own = jnp.pad(jnp.concatenate([tokens, meta], axis=1), ((0, 4), (0, 0)))
-    a32, b16 = line_up(place, [own] + [shift(own, FIRST, by) for by in (1, 2, 3)])
-    near, far = grow(a32, b16)
+    parts = first_gather(jnp.concatenate([tokens, meta], axis=1), core, at)
+    near, far = grow(parts)
 
     weights = (teacher_gate, teacher_up, student_gate, student_up)
     h_near, ab_near = forward(info, near, *weights)
+    far, h_near = lax.optimization_barrier((far, h_near))
     h_far, ab_far = forward(info, far, *weights)
     far_out = down(h_far, student_down, teacher_down)
     near_out = down(h_near, student_down, teacher_down)
 
-    rows48 = shrink(near_out, far_out)
-    part = rows48.astype(BF)
-    for by in (1, 2, 3):
-        rows48 = rows48 + shift(part, FIRST, by).astype(F32)
-    depth = tokens.shape[1]
-    weight = join(a32[:, depth : depth + 1], b16[:, depth : depth + 1]).astype(F32)
-    cotangent = (weight * (weight * rows48) * (1.0 / math.sqrt(total))).astype(BF)
-    c_near, c_far = grow(cotangent[:32], cotangent[32:])
+    depth, scale = tokens.shape[1], 1.0 / math.sqrt(total)
+    cotangent = []
+    for part, rows in zip(parts, shrink(near_out, far_out)):
+        weight = part[:, depth : depth + 1].astype(F32)
+        cotangent.append((weight * (weight * rows) * scale).astype(BF))
+    c_near, c_far = grow(cotangent)
 
     send, keep = backward(
         core.astype(jnp.int32).reshape(1), near + far, c_near + c_far, student_down, h_near, h_far, ab_near, ab_far

time: 281 us -> 218 us (0.78)
  waiting for transfers between devices: 167 us -> 80.3 us
  starting transfers between devices: 44.8 us -> 78.2 us
  local copies, waits for them, and re-layouts: 18 us -> 11.3 us
  Pallas kernels: 44.1 us -> 38.7 us
    ppermute x36 -> x45, waiting for transfers between devices: 163 us -> 76.2 us  [the longest x36 59.5 us: hop(): return lax.ppermute(value, AXES, step_pairs(piece, step))]
    ppermute x36 -> x45, starting transfers between devices: 27.7 us -> 78.1 us  [the longest x36 60.5 us: hop(): return lax.ppermute(value, AXES, step_pairs(piece, step))]
    ppermute x1, starting transfers between devices: 17.1 us -> 0.08 us  [per_device(): got = lax.ppermute(send, 'dp', [(0, 1), (1, 0)])]
    pallas_call x2, Pallas kernels: 18.6 us -> 12 us  [forward(): pl.pallas_call(functools.partial(forward_kernel, count, steps), grid=(ste...]
    unnamed x46 -> x34, local copies, waits for them, and re-layouts: 14.6 us -> 9.33 us
  transfers between devices with their start and end apart: 37 -> 46, of which waited for: 31 -> 29; matrix products, arithmetic and copies ran while one was open for 3% -> 3% of each run, Pallas kernels for 4% -> 5%
where the time goes in v2:
time: 218 us; the launch traced here: 217 us
  waiting for transfers between devices  80.3 us (37%)
  starting transfers between devices  78.2 us (36%)
  Pallas kernels  38.7 us (18%)
  local copies, waits for them, and re-layouts  11.3 us (5%)
  other arithmetic  7.48 us (3%)
    ppermute x36, starting transfers between devices, hop(): return lax.ppermute(value, AXES, step_pairs(piece, step))  60.5 us
    ppermute x36, waiting for transfers between devices, hop(): return lax.ppermute(value, AXES, step_pairs(piece, step))  59.5 us
    ppermute x9, starting transfers between devices, hop_back(): lax.ppermute(value, AXES, [(to, own) for own, to in step_pairs(piece, ste...  17.5 us
    ppermute x9, waiting for transfers between devices, hop_back(): lax.ppermute(value, AXES, [(to, own) for own, to in step_pairs(piece, ste...  16.6 us
    pallas_call x1, Pallas kernels, backward(): pl.pallas_call(functools.partial(backward_kernel, count, half), grid_spec...  14.8 us
    pallas_call x2, Pallas kernels, forward(): pl.pallas_call(functools.partial(forward_kernel, count, steps), grid=(ste...  12 us
    unnamed x34, local copies, waits for them, and re-layouts  9.33 us
    pallas_call x2, Pallas kernels, down(): pl.pallas_call(functools.partial(down_kernel, count), grid=(width // bloc...  6.48 us
  transfers between devices with their start and end apart: 46, of which 29 were waited for; matrix products, arithmetic and copies ran while one was open for 3% of the time, Pallas kernels for 5%

profile of v2, /device:TPU:1, one launch (start us, length us, event | category | flops | bytes accessed | tf_op | source)
XLA Modules:
  0.0 217.1 jit_solution(2815785277951131566)
XLA Ops:
  3.2 3.6 %collective-permute-start.5 = (bf16[8,5248]{1,0:T(8,128)(2,1)S(1)}, bf16[8,5248]{1,0:T(8,128)(2,1)S(1)}, u32[]{:S(2)}, u32[]{:S(2)}) collective-permute-start(bf16[8,5248]{1,0:T(8,128)(2,1)S(1)} %pad.11), channel_id=1, source_target_pairs={{0,4},{1,5},{2,6},{3,7},{4,0},{5,1},{6,2},{7,3},{8,12},{9,13},{10,... | collective-permute-start | bytes 251912 | tf_op jit(solution)/shard_map/ppermute | solution.py:47
  6.9 3.8 %collective-permute-start.10 = (bf16[8,5248]{1,0:T(8,128)(2,1)S(1)}, bf16[8,5248]{1,0:T(8,128)(2,1)S(1)}, u32[]{:S(2)}, u32[]{:S(2)}) collective-permute-start(bf16[8,5248]{1,0:T(8,128)(2,1)S(1)} %pad.12), channel_id=1, source_target_pairs={{0,16},{1,17},{2,18},{3,19},{4,20},{5,21},{6,22},{7,23},{8,24},{9,... | collective-permute-start | bytes 251912 | tf_op jit(solution)/shard_map/ppermute | solution.py:47
  16.4 3.9 %collective-permute-done.1.got = bf16[16,5248]{1,0:T(8,128)(2,1)S(1)} collective-permute-done((bf16[16,5248]{1,0:T(8,128)(2,1)S(1)}, bf16[16,5248]{1,0:T(8,128)(2,1)S(1)}, u32[]{:S(2)}, u32[]{:S(2)}) %collective-permute-start.1) | collective-permute-done | bytes 167968 | tf_op jit(solution)/shard_map/ppermute | solution.py:47
  31.1 3.2 %collective-permute-start.8 = (bf16[32,5248]{1,0:T(8,128)(2,1)S(1)}, bf16[32,5248]{1,0:T(8,128)(2,1)S(1)}, u32[]{:S(2)}, u32[]{:S(2)}) collective-permute-start(bf16[32,5248]{1,0:T(8,128)(2,1)S(1)} %pad_maximum_fusion.13), channel_id=1, source_target_pairs={{0,112},{1,113},{2,114},{3,115},{4,116},{5,117},{6,118},{7,119},{8... | collective-permute-start | bytes 1007624 | tf_op jit(solution)/shard_map/ppermute | solution.py:47
  36.3 3.7 %collective-permute-done.8 = bf16[32,5248]{1,0:T(8,128)(2,1)S(1)} collective-permute-done((bf16[32,5248]{1,0:T(8,128)(2,1)S(1)}, bf16[32,5248]{1,0:T(8,128)(2,1)S(1)}, u32[]{:S(2)}, u32[]{:S(2)}) %collective-permute-start.8) | collective-permute-done | bytes 335904 | tf_op jit(solution)/shard_map/ppermute | solution.py:47
  42.6 8.3 %collective-permute-done.9 = bf16[64,5248]{1,0:T(8,128)(2,1)S(1)} collective-permute-done((bf16[64,5248]{1,0:T(8,128)(2,1)S(1)}, bf16[64,5248]{1,0:T(8,128)(2,1)S(1)}, u32[]{:S(2)}, u32[]{:S(2)}) %collective-permute-start.9) | collective-permute-done | bytes 671776 | tf_op jit(solution)/shard_map/ppermute | solution.py:47
  52.9 3.4 %collective-permute-start.15 = (bf16[128,5248]{1,0:T(8,128)(2,1)}, bf16[128,5248]{1,0:T(8,128)(2,1)}, u32[]{:S(2)}, u32[]{:S(2)}) collective-permute-start(bf16[128,5248]{1,0:T(8,128)(2,1)} %pad_maximum_fusion.refs_0_.refs_3_), channel_id=1, source_target_pairs={{0,112},{1,113},{2,114},{3,115},{4,116},{5,117},{6,118},{7,119},{8... | collective-permute-start | bytes 4030472 | tf_op jit(solution)/shard_map/ppermute | solution.py:47
  62.5 5.9 %shard_map.178 = (bf16[384,384]{1,0:T(8,128)(2,1)S(1)}, f32[384,256]{1,0:T(8,128)S(1)}) custom-call(s32[5]{0:T(128)S(1)} %pad_add_fusion.info, bf16[128,5248]{1,0:T(8,128)(2,1)} %pad_maximum_fusion.refs_0_.refs_3_, bf16[128,5248]{1,0:T(8,128)(2,1)S(1)} %pad_maximum_fusion.1.refs_1_.refs_4_, bf16[128,5248]{1,0:T(8,128)(2,1)S(1)} %pad_maximum_fusion.2.refs_2_.refs_5_, ...), custom_call_target="tpu_custom_call" | custom-call | flops 3019898880 | bytes 11796480 | tf_op jit(solution)/shard_map/pallas_call | solution.py:163
  72.5 6.1 %shard_map.180 = (bf16[384,384]{1,0:T(8,128)(2,1)S(1)}, f32[384,256]{1,0:T(8,128)S(1)}) custom-call(s32[5]{0:T(128)S(1)} %pad_add_fusion.info, bf16[128,5248]{1,0:T(8,128)(2,1)} %collective-permute-done.15.refs_0_.refs_3_, bf16[128,5248]{1,0:T(8,128)(2,1)} %collective-permute-done.16.refs_1_.refs_4_, ...), custom_call_target="tpu_custom_call" | custom-call | flops 3019898880 | bytes 11796480 | tf_op jit(solution)/shard_map/pallas_call | solution.py:163
  78.6 3.2 %shard_map.181 = (bf16[128,5120]{1,0:T(8,128)(2,1)S(1)}, bf16[128,5120]{1,0:T(8,128)(2,1)S(1)}, bf16[128,5120]{1,0:T(8,128)(2,1)S(1)}) custom-call(bf16[384,384]{1,0:T(8,128)(2,1)S(1)} %get-tuple-element.25.h_ref.refs_14_, bf16[128,5120]{1,0:T(8,128)(2,1)S(1)} %copy-done.9, bf16[256,5120]{1,0:T(8,128)(2,1)S(1)} %copy-done.10), custom_call_target="tpu_custom_call" | custom-call | flops 1509949440 | bytes 7864320 | tf_op jit(solution)/shard_map/pallas_call | solution.py:188
  86.5 3.2 %shard_map.179 = (bf16[128,5120]{1,0:T(8,128)(2,1)S(1)}, bf16[128,5120]{1,0:T(8,128)(2,1)S(1)}, bf16[128,5120]{1,0:T(8,128)(2,1)S(1)}) custom-call(bf16[384,384]{1,0:T(8,128)(2,1)S(1)} %get-tuple-element.23.h_ref.refs_13_, bf16[128,5120]{1,0:T(8,128)(2,1)S(1)} %copy-done.9, bf16[256,5120]{1,0:T(8,128)(2,1)S(1)} %copy-done.10), custom_call_target="tpu_custom_call" | custom-call | flops 1509949440 | bytes 7864320 | tf_op jit(solution)/shard_map/pallas_call | solution.py:188
  89.7 9.5 %collective-permute-done.34 = bf16[128,5120]{1,0:T(8,128)(2,1)S(1)} collective-permute-done((bf16[128,5120]{1,0:T(8,128)(2,1)S(1)}, bf16[128,5120]{1,0:T(8,128)(2,1)S(1)}, u32[]{:S(2)}, u32[]{:S(2)}) %collective-permute-start.34) | collective-permute-done | bytes 1310752 | tf_op jit(solution)/shard_map/ppermute | solution.py:51
  99.6 3.1 %collective-permute-start.35 = (bf16[64,5120]{1,0:T(8,128)(2,1)S(1)}, bf16[64,5120]{1,0:T(8,128)(2,1)S(1)}, u32[]{:S(2)}, u32[]{:S(2)}) collective-permute-start(bf16[64,5120]{1,0:T(8,128)(2,1)S(1)} %get-tuple-element.41), channel_id=1, source_target_pairs={{4,0},{5,1},{6,2},{7,3},{0,4},{1,5},{2,6},{3,7},{12,8},{13,9},{14,... | collective-permute-start | bytes 1966088 | tf_op jit(solution)/shard_map/ppermute | solution.py:51
  106.8 3.9 %collective-permute-done.35 = bf16[64,5120]{1,0:T(8,128)(2,1)S(1)} collective-permute-done((bf16[64,5120]{1,0:T(8,128)(2,1)S(1)}, bf16[64,5120]{1,0:T(8,128)(2,1)S(1)}, u32[]{:S(2)}, u32[]{:S(2)}) %collective-permute-start.35) | collective-permute-done | bytes 655392 | tf_op jit(solution)/shard_map/ppermute | solution.py:51
  110.7 3.5 %collective-permute-start.36 = (bf16[32,5120]{1,0:T(8,128)(2,1)S(1)}, bf16[32,5120]{1,0:T(8,128)(2,1)S(1)}, u32[]{:S(2)}, u32[]{:S(2)}) collective-permute-start(bf16[32,5120]{1,0:T(8,128)(2,1)S(1)} %fusion), channel_id=1, source_target_pairs={{67,0},{66,1},{65,2},{64,3},{71,4},{70,5},{69,6},{68,7},{75,8},{74... | collective-permute-start | bytes 983048 | tf_op jit(solution)/shard_map/ppermute | solution.py:51
  140.8 3.5 %collective-permute-start.40 = (bf16[32,5120]{1,0:T(8,128)(2,1)S(1)}, bf16[32,5120]{1,0:T(8,128)(2,1)S(1)}, u32[]{:S(2)}, u32[]{:S(2)}) collective-permute-start(bf16[32,5120]{1,0:T(8,128)(2,1)S(1)} %multiply_convert_fusion), channel_id=1, source_target_pairs={{0,67},{1,66},{2,65},{3,64},{4,71},{5,70},{6,69},{7,68},{8,75},{9,... | collective-permute-start | bytes 983048 | tf_op jit(solution)/shard_map/ppermute | solution.py:47
  144.5 6.0 %collective-permute-start.24 = (bf16[32,5120]{1,0:T(8,128)(2,1)S(1)}, bf16[32,5120]{1,0:T(8,128)(2,1)S(1)}, u32[]{:S(2)}, u32[]{:S(2)}) collective-permute-start(bf16[32,5120]{1,0:T(8,128)(2,1)S(1)} %multiply_convert_fusion.2), channel_id=1, source_target_pairs={{0,76},{1,77},{2,78},{3,79},{4,72},{5,73},{6,74},{7,75},{8,68},{9,... | collective-permute-start | bytes 983048 | tf_op jit(solution)/shard_map/ppermute | solution.py:47
  150.8 4.7 %collective-permute-done.24 = bf16[32,5120]{1,0:T(8,128)(2,1)S(1)} collective-permute-done((bf16[32,5120]{1,0:T(8,128)(2,1)S(1)}, bf16[32,5120]{1,0:T(8,128)(2,1)S(1)}, u32[]{:S(2)}, u32[]{:S(2)}) %collective-permute-start.24) | collective-permute-done | bytes 327712 | tf_op jit(solution)/shard_map/ppermute | solution.py:47
  155.6 3.9 %collective-permute-start.25 = (bf16[64,5120]{1,0:T(8,128)(2,1)S(1)}, bf16[64,5120]{1,0:T(8,128)(2,1)S(1)}, u32[]{:S(2)}, u32[]{:S(2)}) collective-permute-start(bf16[64,5120]{1,0:T(8,128)(2,1)S(1)} %pad_maximum_fusion.9), channel_id=1, source_target_pairs={{0,16},{1,17},{2,18},{3,19},{4,20},{5,21},{6,22},{7,23},{8,24},{9,... | collective-permute-start | bytes 1966088 | tf_op jit(solution)/shard_map/ppermute | solution.py:47
  173.0 3.1 %collective-permute-start.44 = (bf16[128,5120]{1,0:T(8,128)(2,1)S(1)}, bf16[128,5120]{1,0:T(8,128)(2,1)S(1)}, u32[]{:S(2)}, u32[]{:S(2)}) collective-permute-start(bf16[128,5120]{1,0:T(8,128)(2,1)S(1)} %pad_maximum_fusion.5.refs_8_), channel_id=1, source_target_pairs={{0,76},{1,77},{2,78},{3,79},{4,72},{5,73},{6,74},{7,75},{8,68},{9,... | collective-permute-start | bytes 3932168 | tf_op jit(solution)/shard_map/ppermute | solution.py:47
  176.1 10.4 %collective-permute-done.42.refs_9_ = bf16[128,5120]{1,0:T(8,128)(2,1)S(1)} collective-permute-done((bf16[128,5120]{1,0:T(8,128)(2,1)S(1)}, bf16[128,5120]{1,0:T(8,128)(2,1)S(1)}, u32[]{:S(2)}, u32[]{:S(2)}) %collective-permute-start.42) | collective-permute-done | bytes 1310752 | tf_op jit(solution)/shard_map/ppermute | solution.py:47
  192.6 14.8 %shard_map.182 = (bf16[384,2560]{1,0:T(8,128)(2,1)}, f32[384,2560]{1,0:T(8,128)}) custom-call(s32[1]{0:T(128)} %bitcast.core, bf16[128,5248]{1,0:T(8,128)(2,1)} %pad_maximum_fusion.refs_0_.refs_3_, bf16[128,5248]{1,0:T(8,128)(2,1)} %copy-done, bf16[128,5248]{1,0:T(8,128)(2,1)} %copy-done.1, bf16[128,5248]{1,0:T(8,128)(2,1)} %collective-permute-done.15.refs_0_.refs_3_, ...), custom_call_target="tpu_custom_call" | custom-call | flops 4026531840 | bytes 23592960 | tf_op jit(solution)/shard_map/pallas_call | solution.py:254
  207.5 4.2 %collective-permute-done.45.got = bf16[384,2560]{1,0:T(8,128)(2,1)S(1)} collective-permute-done((bf16[384,2560]{1,0:T(8,128)(2,1)}, bf16[384,2560]{1,0:T(8,128)(2,1)S(1)}, u32[]{:S(2)}, u32[]{:S(2)}) %collective-permute-start.45) | collective-permute-done | bytes 1966112 | tf_op jit(solution)/shard_map/ppermute | solution.py:337
  213.8 3.3 %shard_map.183 = (f32[2560,128]{1,0:T(8,128)}, f32[2560,128]{1,0:T(8,128)}, f32[128,2560]{1,0:T(8,128)}) custom-call(f32[384,2560]{1,0:T(8,128)S(1)} %copy-done.8, bf16[384,2560]{1,0:T(8,128)(2,1)S(1)} %collective-permute-done.45.got), custom_call_target="tpu_custom_call" | custom-call | tf_op jit(solution)/shard_map/pallas_call | solution.py:287
  (165 shorter events, 93.5 us)
Async XLA Ops:
  3.2 13.1 %collective-permute-start.5 = (bf16[8,5248]{1,0:T(8,128)(2,1)S(1)}, bf16[8,5248]{1,0:T(8,128)(2,1)S(1)}, u32[]{:S(2)}, u32[]{:S(2)}) collective-permute-start(bf16[8,5248]{1,0:T(8,128)(2,1)S(1)} %pad.11), channel_id=1, source_target_pairs={{0,4},{1,5},{2,6},{3,7},{4,0},{5,1},{6,2},{7,3},{8,12},{9,13},{10,... | collective-permute-start | bytes 251912 | tf_op jit(solution)/shard_map/ppermute | solution.py:47
  6.9 9.3 %collective-permute-start.10 = (bf16[8,5248]{1,0:T(8,128)(2,1)S(1)}, bf16[8,5248]{1,0:T(8,128)(2,1)S(1)}, u32[]{:S(2)}, u32[]{:S(2)}) collective-permute-start(bf16[8,5248]{1,0:T(8,128)(2,1)S(1)} %pad.12), channel_id=1, source_target_pairs={{0,16},{1,17},{2,18},{3,19},{4,20},{5,21},{6,22},{7,23},{8,24},{9,... | collective-permute-start | bytes 251912 | tf_op jit(solution)/shard_map/ppermute | solution.py:47
  28.6 11.6 %collective-permute-start.13 = (bf16[32,5248]{1,0:T(8,128)(2,1)S(1)}, bf16[32,5248]{1,0:T(8,128)(2,1)S(1)}, u32[]{:S(2)}, u32[]{:S(2)}) collective-permute-start(bf16[32,5248]{1,0:T(8,128)(2,1)S(1)} %pad_maximum_fusion.14), channel_id=1, source_target_pairs={{0,67},{1,66},{2,65},{3,64},{4,71},{5,70},{6,69},{7,68},{8,75},{9,... | collective-permute-start | bytes 1007624 | tf_op jit(solution)/shard_map/ppermute | solution.py:47
  35.2 16.2 %collective-permute-start.4 = (bf16[64,5248]{1,0:T(8,128)(2,1)S(1)}, bf16[64,5248]{1,0:T(8,128)(2,1)S(1)}, u32[]{:S(2)}, u32[]{:S(2)}) collective-permute-start(bf16[64,5248]{1,0:T(8,128)(2,1)S(1)} %pad_maximum_fusion.6), channel_id=1, source_target_pairs={{0,16},{1,17},{2,18},{3,19},{4,20},{5,21},{6,22},{7,23},{8,24},{9,... | collective-permute-start | bytes 2015240 | tf_op jit(solution)/shard_map/ppermute | solution.py:47
  40.1 10.9 %collective-permute-start.9 = (bf16[64,5248]{1,0:T(8,128)(2,1)S(1)}, bf16[64,5248]{1,0:T(8,128)(2,1)S(1)}, u32[]{:S(2)}, u32[]{:S(2)}) collective-permute-start(bf16[64,5248]{1,0:T(8,128)(2,1)S(1)} %pad_maximum_fusion.7), channel_id=1, source_target_pairs={{0,1},{1,0},{2,3},{3,2},{4,5},{5,4},{6,7},{7,6},{8,9},{9,8},{10,11... | collective-permute-start | bytes 2015240 | tf_op jit(solution)/shard_map/ppermute | solution.py:47
  40.2 11.0 %collective-permute-start.14 = (bf16[64,5248]{1,0:T(8,128)(2,1)S(1)}, bf16[64,5248]{1,0:T(8,128)(2,1)S(1)}, u32[]{:S(2)}, u32[]{:S(2)}) collective-permute-start(bf16[64,5248]{1,0:T(8,128)(2,1)S(1)} %pad_maximum_fusion.8), channel_id=1, source_target_pairs={{0,4},{1,5},{2,6},{3,7},{4,0},{5,1},{6,2},{7,3},{8,12},{9,13},{10,... | collective-permute-start | bytes 2015240 | tf_op jit(solution)/shard_map/ppermute | solution.py:47
  51.1 18.8 %collective-permute-start.16 = (bf16[128,5248]{1,0:T(8,128)(2,1)S(1)}, bf16[128,5248]{1,0:T(8,128)(2,1)}, u32[]{:S(2)}, u32[]{:S(2)}) collective-permute-start(bf16[128,5248]{1,0:T(8,128)(2,1)S(1)} %pad_maximum_fusion.1.refs_1_.refs_4_), channel_id=1, source_target_pairs={{0,67},{1,66},{2,65},{3,64},{4,71},{5,70},{6,69},{7,68},{8,75},{9,... | collective-permute-start | bytes 4030472 | tf_op jit(solution)/shard_map/ppermute | solution.py:47
  51.3 19.5 %collective-permute-start.17 = (bf16[128,5248]{1,0:T(8,128)(2,1)S(1)}, bf16[128,5248]{1,0:T(8,128)(2,1)}, u32[]{:S(2)}, u32[]{:S(2)}) collective-permute-start(bf16[128,5248]{1,0:T(8,128)(2,1)S(1)} %pad_maximum_fusion.2.refs_2_.refs_5_), channel_id=1, source_target_pairs={{0,76},{1,77},{2,78},{3,79},{4,72},{5,73},{6,74},{7,75},{8,68},{9,... | collective-permute-start | bytes 4030472 | tf_op jit(solution)/shard_map/ppermute | solution.py:47
  52.9 19.7 %collective-permute-start.15 = (bf16[128,5248]{1,0:T(8,128)(2,1)}, bf16[128,5248]{1,0:T(8,128)(2,1)}, u32[]{:S(2)}, u32[]{:S(2)}) collective-permute-start(bf16[128,5248]{1,0:T(8,128)(2,1)} %pad_maximum_fusion.refs_0_.refs_3_), channel_id=1, source_target_pairs={{0,112},{1,113},{2,114},{3,115},{4,116},{5,117},{6,118},{7,119},{8... | collective-permute-start | bytes 4030472 | tf_op jit(solution)/shard_map/ppermute | solution.py:47
  81.9 17.4 %collective-permute-start.34 = (bf16[128,5120]{1,0:T(8,128)(2,1)S(1)}, bf16[128,5120]{1,0:T(8,128)(2,1)S(1)}, u32[]{:S(2)}, u32[]{:S(2)}) collective-permute-start(bf16[128,5120]{1,0:T(8,128)(2,1)S(1)} %get-tuple-element.30), channel_id=1, source_target_pairs={{76,0},{77,1},{78,2},{79,3},{72,4},{73,5},{74,6},{75,7},{68,8},{69... | collective-permute-start | bytes 3932168 | tf_op jit(solution)/shard_map/ppermute | solution.py:51
  84.0 20.4 %collective-permute-start.18 = (bf16[128,5120]{1,0:T(8,128)(2,1)S(1)}, bf16[128,5120]{1,0:T(8,128)(2,1)S(1)}, u32[]{:S(2)}, u32[]{:S(2)}) collective-permute-start(bf16[128,5120]{1,0:T(8,128)(2,1)S(1)} %get-tuple-element.26), channel_id=1, source_target_pairs={{112,0},{113,1},{114,2},{115,3},{116,4},{117,5},{118,6},{119,7},{1... | collective-permute-start | bytes 3932168 | tf_op jit(solution)/shard_map/ppermute | solution.py:51
  85.2 17.6 %collective-permute-start.26 = (bf16[128,5120]{1,0:T(8,128)(2,1)S(1)}, bf16[128,5120]{1,0:T(8,128)(2,1)S(1)}, u32[]{:S(2)}, u32[]{:S(2)}) collective-permute-start(bf16[128,5120]{1,0:T(8,128)(2,1)S(1)} %get-tuple-element.28), channel_id=1, source_target_pairs={{67,0},{66,1},{65,2},{64,3},{71,4},{70,5},{69,6},{68,7},{75,8},{74... | collective-permute-start | bytes 3932168 | tf_op jit(solution)/shard_map/ppermute | solution.py:51
  99.6 11.1 %collective-permute-start.35 = (bf16[64,5120]{1,0:T(8,128)(2,1)S(1)}, bf16[64,5120]{1,0:T(8,128)(2,1)S(1)}, u32[]{:S(2)}, u32[]{:S(2)}) collective-permute-start(bf16[64,5120]{1,0:T(8,128)(2,1)S(1)} %get-tuple-element.41), channel_id=1, source_target_pairs={{4,0},{5,1},{6,2},{7,3},{0,4},{1,5},{2,6},{3,7},{12,8},{13,9},{14,... | collective-permute-start | bytes 1966088 | tf_op jit(solution)/shard_map/ppermute | solution.py:51
  103.1 11.1 %collective-permute-start.27 = (bf16[64,5120]{1,0:T(8,128)(2,1)S(1)}, bf16[64,5120]{1,0:T(8,128)(2,1)S(1)}, u32[]{:S(2)}, u32[]{:S(2)}) collective-permute-start(bf16[64,5120]{1,0:T(8,128)(2,1)S(1)} %get-tuple-element.43), channel_id=1, source_target_pairs={{1,0},{0,1},{3,2},{2,3},{5,4},{4,5},{7,6},{6,7},{9,8},{8,9},{11,10... | collective-permute-start | bytes 1966088 | tf_op jit(solution)/shard_map/ppermute | solution.py:51
  104.7 10.7 %collective-permute-start.19 = (bf16[64,5120]{1,0:T(8,128)(2,1)S(1)}, bf16[64,5120]{1,0:T(8,128)(2,1)S(1)}, u32[]{:S(2)}, u32[]{:S(2)}) collective-permute-start(bf16[64,5120]{1,0:T(8,128)(2,1)S(1)} %get-tuple-element.45), channel_id=1, source_target_pairs={{16,0},{17,1},{18,2},{19,3},{20,4},{21,5},{22,6},{23,7},{24,8},{25... | collective-permute-start | bytes 1966088 | tf_op jit(solution)/shard_map/ppermute | solution.py:51
  135.0 15.5 %collective-permute-start.31 = (bf16[32,5120]{1,0:T(8,128)(2,1)S(1)}, bf16[32,5120]{1,0:T(8,128)(2,1)S(1)}, u32[]{:S(2)}, u32[]{:S(2)}) collective-permute-start(bf16[32,5120]{1,0:T(8,128)(2,1)S(1)} %fusion.10), channel_id=1, source_target_pairs={{0,4},{1,5},{2,6},{3,7},{4,0},{5,1},{6,2},{7,3},{8,12},{9,13},{10,... | collective-permute-start | bytes 983048 | tf_op jit(solution)/shard_map/ppermute | solution.py:47
  140.8 21.0 %collective-permute-start.40 = (bf16[32,5120]{1,0:T(8,128)(2,1)S(1)}, bf16[32,5120]{1,0:T(8,128)(2,1)S(1)}, u32[]{:S(2)}, u32[]{:S(2)}) collective-permute-start(bf16[32,5120]{1,0:T(8,128)(2,1)S(1)} %multiply_convert_fusion), channel_id=1, source_target_pairs={{0,67},{1,66},{2,65},{3,64},{4,71},{5,70},{6,69},{7,68},{8,75},{9,... | collective-permute-start | bytes 983048 | tf_op jit(solution)/shard_map/ppermute | solution.py:47
  144.5 11.1 %collective-permute-start.24 = (bf16[32,5120]{1,0:T(8,128)(2,1)S(1)}, bf16[32,5120]{1,0:T(8,128)(2,1)S(1)}, u32[]{:S(2)}, u32[]{:S(2)}) collective-permute-start(bf16[32,5120]{1,0:T(8,128)(2,1)S(1)} %multiply_convert_fusion.2), channel_id=1, source_target_pairs={{0,76},{1,77},{2,78},{3,79},{4,72},{5,73},{6,74},{7,75},{8,68},{9,... | collective-permute-start | bytes 983048 | tf_op jit(solution)/shard_map/ppermute | solution.py:47
  155.6 11.9 %collective-permute-start.25 = (bf16[64,5120]{1,0:T(8,128)(2,1)S(1)}, bf16[64,5120]{1,0:T(8,128)(2,1)S(1)}, u32[]{:S(2)}, u32[]{:S(2)}) collective-permute-start(bf16[64,5120]{1,0:T(8,128)(2,1)S(1)} %pad_maximum_fusion.9), channel_id=1, source_target_pairs={{0,16},{1,17},{2,18},{3,19},{4,20},{5,21},{6,22},{7,23},{8,24},{9,... | collective-permute-start | bytes 1966088 | tf_op jit(solution)/shard_map/ppermute | solution.py:47
  159.5 10.7 %collective-permute-start.33 = (bf16[64,5120]{1,0:T(8,128)(2,1)S(1)}, bf16[64,5120]{1,0:T(8,128)(2,1)S(1)}, u32[]{:S(2)}, u32[]{:S(2)}) collective-permute-start(bf16[64,5120]{1,0:T(8,128)(2,1)S(1)} %pad_maximum_fusion.10), channel_id=1, source_target_pairs={{0,1},{1,0},{2,3},{3,2},{4,5},{5,4},{6,7},{7,6},{8,9},{9,8},{10,11... | collective-permute-start | bytes 1966088 | tf_op jit(solution)/shard_map/ppermute | solution.py:47
  161.8 11.1 %collective-permute-start.41 = (bf16[64,5120]{1,0:T(8,128)(2,1)S(1)}, bf16[64,5120]{1,0:T(8,128)(2,1)S(1)}, u32[]{:S(2)}, u32[]{:S(2)}) collective-permute-start(bf16[64,5120]{1,0:T(8,128)(2,1)S(1)} %pad_maximum_fusion.11), channel_id=1, source_target_pairs={{0,4},{1,5},{2,6},{3,7},{4,0},{5,1},{6,2},{7,3},{8,12},{9,13},{10,... | collective-permute-start | bytes 1966088 | tf_op jit(solution)/shard_map/ppermute | solution.py:47
  167.5 19.0 %collective-permute-start.42 = (bf16[128,5120]{1,0:T(8,128)(2,1)S(1)}, bf16[128,5120]{1,0:T(8,128)(2,1)S(1)}, u32[]{:S(2)}, u32[]{:S(2)}) collective-permute-start(bf16[128,5120]{1,0:T(8,128)(2,1)S(1)} %pad_maximum_fusion.3.refs_6_), channel_id=1, source_target_pairs={{0,112},{1,113},{2,114},{3,115},{4,116},{5,117},{6,118},{7,119},{8... | collective-permute-start | bytes 3932168 | tf_op jit(solution)/shard_map/ppermute | solution.py:47
  170.3 18.3 %collective-permute-start.43 = (bf16[128,5120]{1,0:T(8,128)(2,1)S(1)}, bf16[128,5120]{1,0:T(8,128)(2,1)S(1)}, u32[]{:S(2)}, u32[]{:S(2)}) collective-permute-start(bf16[128,5120]{1,0:T(8,128)(2,1)S(1)} %pad_maximum_fusion.4.refs_7_), channel_id=1, source_target_pairs={{0,67},{1,66},{2,65},{3,64},{4,71},{5,70},{6,69},{7,68},{8,75},{9,... | collective-permute-start | bytes 3932168 | tf_op jit(solution)/shard_map/ppermute | solution.py:47
  173.0 18.5 %collective-permute-start.44 = (bf16[128,5120]{1,0:T(8,128)(2,1)S(1)}, bf16[128,5120]{1,0:T(8,128)(2,1)S(1)}, u32[]{:S(2)}, u32[]{:S(2)}) collective-permute-start(bf16[128,5120]{1,0:T(8,128)(2,1)S(1)} %pad_maximum_fusion.5.refs_8_), channel_id=1, source_target_pairs={{0,76},{1,77},{2,78},{3,79},{4,72},{5,73},{6,74},{7,75},{8,68},{9,... | collective-permute-start | bytes 3932168 | tf_op jit(solution)/shard_map/ppermute | solution.py:47
  (39 other events, 238.6 us)

commit v3 on v2

--- a/solution.py
+++ b/solution.py
@@ -79,7 +79,7 @@
         sums.append(mine)
     for step in (2, 1, 0):
         sums = [add(v, hop(v.astype(BF), p, step)) for p, v in enumerate(sums)]
-    return sums
+    return lax.optimization_barrier(sums)
 
 
 def line_up_kernel(place_ref, mine, got, out):
@@ -101,7 +101,7 @@
         out_shape=jax.ShapeDtypeStruct((16, mine.shape[1]), BF),
         in_specs=[pl.BlockSpec(memory_space=pltpu.SMEM), vmem, vmem],
         out_specs=vmem,
-        compiler_params=pltpu.CompilerParams(vmem_limit_bytes=32 << 20),
+        compiler_params=pltpu.CompilerParams(vmem_limit_bytes=16 << 20),
     )(places, mine, got)
 
 
@@ -122,7 +122,7 @@
 
 def forward_kernel(count, steps, info, *refs):
     xs, metas = refs[:count], refs[count : 2 * count]
-    tg, tu, sg, su, h_ref, ab_ref, acc = refs[2 * count :]
+    tg, tu, sg, su, h_ref, ht_ref, ab_ref, acc = refs[2 * count :]
     step = pl.program_id(0)
     x = jnp.concatenate([r[...] for r in xs], axis=0)
     w = jnp.concatenate([tg[...], tu[...], sg[...], su[...]], axis=1)
@@ -150,7 +150,9 @@
         gate, up = acc[:, 512:640], acc[:, 640:768]
         sig = jax.nn.sigmoid(gate)
         silu = gate * sig
-        h_ref[:, 0:128] = jnp.where(mask_s, silu * up, 0.0).astype(BF)
+        hid_s = jnp.where(mask_s, silu * up, 0.0)
+        h_ref[:, 0:128] = hid_s.astype(BF)
+        ht_ref[...] = hid_s.T.astype(BF)
         ab_ref[:, 0:128] = jnp.where(mask_s, up * sig * (1.0 + gate * (1.0 - sig)), 0.0)
         ab_ref[:, 128:256] = jnp.where(mask_s, silu, 0.0)
 
@@ -163,14 +165,22 @@
     return pl.pallas_call(
         functools.partial(forward_kernel, count, steps),
         grid=(steps,),
-        out_shape=[jax.ShapeDtypeStruct((rows, 384), BF), jax.ShapeDtypeStruct((rows, 256), F32)],
+        out_shape=[
+            jax.ShapeDtypeStruct((rows, 384), BF),
+            jax.ShapeDtypeStruct((128, rows), BF),
+            jax.ShapeDtypeStruct((rows, 256), F32),
+        ],
         in_specs=[pl.BlockSpec(memory_space=pltpu.SMEM)]
         + [pl.BlockSpec((128, block), lambda k: (0, k))] * count
         + [pl.BlockSpec((128, META), lambda k: (0, depth // META))] * count
         + [pl.BlockSpec((block, w.shape[1]), at_k) for w in (tg, tu, sg, su)],
-        out_specs=[pl.BlockSpec((rows, 384), lambda k: (0, 0)), pl.BlockSpec((rows, 256), lambda k: (0, 0))],
+        out_specs=[
+            pl.BlockSpec((rows, 384), lambda k: (0, 0)),
+            pl.BlockSpec((128, rows), lambda k: (0, 0)),
+            pl.BlockSpec((rows, 256), lambda k: (0, 0)),
+        ],
         scratch_shapes=[pltpu.VMEM((rows, 768), F32)],
-        compiler_params=pltpu.CompilerParams(vmem_limit_bytes=40 << 20),
+        compiler_params=pltpu.CompilerParams(vmem_limit_bytes=16 << 20),
         cost_estimate=pl.CostEstimate(flops=2 * rows * depth * 768, bytes_accessed=2 * depth * (rows + 768), transcendentals=0),
     )(info, *chunks, *chunks, tg, tu, sg, su)
 
@@ -195,103 +205,171 @@
             pl.BlockSpec((256, block), lambda n: (0, n)),
         ],
         out_specs=[pl.BlockSpec((128, block), lambda n: (0, n))] * count,
-        compiler_params=pltpu.CompilerParams(vmem_limit_bytes=40 << 20),
+        compiler_params=pltpu.CompilerParams(vmem_limit_bytes=16 << 20),
         cost_estimate=pl.CostEstimate(flops=2 * rows * width * 384, bytes_accessed=2 * width * (rows + 384), transcendentals=0),
     )(hidden, sd, td)
 
 
-def backward_kernel(count, half, core, *refs):
-    xs, cs = refs[:count], refs[count : 2 * count]
-    sd, h1, h2, ab1, ab2, send, keep, acc, gt, ht = refs[2 * count :]
+BLOCK = 1280
+
+
+def into(acc, step, part):
+    @pl.when(step == 0)
+    def _():
+        acc[...] = part
+
+    @pl.when(step > 0)
+    def _():
+        acc[...] += part
+
+
+def dhidden_part(cs, sd):
+    c = jnp.concatenate([r[...] for r in cs], axis=0)
+    return lax.dot_general(c, sd[...], (((1,), (1,)), ((), ())), preferred_element_type=F32)
+
+
+def dgates(acc, ab):
+    return jnp.concatenate([acc[...] * ab[:, 0:128], acc[...] * ab[:, 128:256]], axis=1).astype(BF)
+
+
+def dhidden_kernel(steps, *refs):
+    cs, (sd, ab, g, acc) = refs[:-4], refs[-4:]
     step = pl.program_id(0)
+    into(acc, step, dhidden_part(cs, sd))
+
+    @pl.when(step == steps - 1)
+    def _():
+        g[...] = dgates(acc, ab)
+
+
+def dhidden(cs, sd, ab):
+    rows, width = 128 * len(cs), sd.shape[1]
+    steps = width // BLOCK
+    wide = pl.BlockSpec((128, BLOCK), lambda k: (0, k))
+    whole = pl.BlockSpec((rows, 256), lambda k: (0, 0))
+    return pl.pallas_call(
+        functools.partial(dhidden_kernel, steps),
+        grid=(steps,),
+        out_shape=jax.ShapeDtypeStruct((rows, 256), BF),
+        in_specs=[wide] * len(cs) + [wide, whole],
+        out_specs=whole,
+        scratch_shapes=[pltpu.VMEM((rows, 128), F32)],
+        compiler_params=pltpu.CompilerParams(vmem_limit_bytes=16 << 20),
+        cost_estimate=pl.CostEstimate(flops=2 * rows * width * 128, bytes_accessed=2 * rows * width, transcendentals=0),
+    )(*cs, sd, ab)
+
+
+def turn_kernel(*refs):
+    xs, out = refs[:-1], refs[-1]
+    for i, r in enumerate(xs):
+        out[:, 128 * i : 128 * (i + 1)] = r[...].T
+
+
+def turn(xs, width):
+    rows, block = 128 * len(xs), 1280
+    return pl.pallas_call(
+        turn_kernel,
+        grid=(width // block,),
+        out_shape=jax.ShapeDtypeStruct((width, rows), BF),
+        in_specs=[pl.BlockSpec((128, block), lambda n: (0, n))] * len(xs),
+        out_specs=pl.BlockSpec((block, rows), lambda n: (n, 0)),
+        compiler_params=pltpu.CompilerParams(vmem_limit_bytes=16 << 20),
+        cost_estimate=pl.CostEstimate(flops=0, bytes_accessed=4 * rows * width, transcendentals=0),
+    )(*xs)
+
+
+def products(xt, cs, g, ht):
     c = jnp.concatenate([r[...] for r in cs], axis=0)
+    return jnp.dot(xt[...], g, preferred_element_type=F32), jnp.dot(ht, c, preferred_element_type=F32)
+
+
+def send_kernel(half, core, *refs):
+    cs = refs[0:6]
+    xt, sd, g1, ht1, ht2, ab, tall, low, g2, acc = refs[6:]
+    step = pl.program_id(0)
 
     @pl.when(step < 2 * half)
     def _():
-        part = lax.dot_general(c, sd[...], (((1,), (1,)), ((), ())), preferred_element_type=F32)
-
-        @pl.when(step == 0)
-        def _():
-            acc[...] = part
-
-        @pl.when(step > 0)
-        def _():
-            acc[...] += part
+        into(acc, step, dhidden_part(cs[3:], sd))
 
     @pl.when(step == 2 * half - 1)
     def _():
-        ab = jnp.concatenate([ab1[...], ab2[...]], axis=0)
-        gt[0:128, :] = (acc[...] * ab[:, 0:128]).T.astype(BF)
-        gt[128:256, :] = (acc[...] * ab[:, 128:256]).T.astype(BF)
-        ht[...] = jnp.concatenate([h1[...], h2[...]], axis=0).astype(F32).T.astype(BF)
+        g2[...] = dgates(acc, ab)
 
     @pl.when(step >= 2 * half)
     def _():
-        x = jnp.concatenate([r[...] for r in xs], axis=0)
-        out = jnp.concatenate(
-            [jnp.dot(gt[...], x, preferred_element_type=F32), jnp.dot(ht[...], c, preferred_element_type=F32)],
-            axis=0,
-        )
-
-        @pl.when(step < 3 * half)
-        def _():
-            send[...] = out.astype(BF)
-
-        @pl.when(step >= 3 * half)
-        def _():
-            keep[...] = out
-
-
-def backward(core, xs, cs, sd, h1, h2, ab1, ab2):
-    count, width = len(xs), sd.shape[1]
-    rows, block = 128 * count, 1280
-    half = width // block // 2
-    turn = lambda s, core: lax.rem(s + (1 - core[0]) * half, 2 * half)
-    x_at = lambda s, core: (0, turn(jnp.maximum(s, 2 * half), core))
-    c_at = lambda s, core: (0, turn(s, core))
-    d_at = lambda s, core: (0, turn(jnp.minimum(s, 2 * half - 1), core))
-    whole = lambda s, core: (0, 0)
-    return pl.pallas_call(
-        functools.partial(backward_kernel, count, half),
+        g = jnp.concatenate([g1[...], g2[...]], axis=0)
+        ht = jnp.concatenate([ht1[...], ht2[...]], axis=1)
+        up, down = products(xt, cs, g, ht)
+        tall[...] = up.astype(BF)
+        low[...] = down.astype(BF)
+
+
+def send_half(core, xt, cs, sd, g1, ht1, ht2, ab):
+    width = sd.shape[1]
+    half = width // BLOCK // 2
+    theirs = lambda s, core: (1 - core[0]) * half + jnp.maximum(s - 2 * half, 0)
+    at = lambda s, core: (0, theirs(s, core))
+    far_at = lambda s, core: (0, jnp.where(s < 2 * half, s, theirs(s, core)))
+    out_at = lambda s: jnp.maximum(s - 2 * half, 0)
+    fixed = lambda *shape: pl.BlockSpec(shape, lambda s, core: (0, 0))
+    return pl.pallas_call(
+        functools.partial(send_kernel, half),
         grid_spec=pltpu.PrefetchScalarGridSpec(
             num_scalar_prefetch=1,
-            grid=(4 * half,),
-            in_specs=[pl.BlockSpec((128, block), x_at)] * count
-            + [pl.BlockSpec((128, block), c_at)] * count
-            + [pl.BlockSpec((128, block), d_at)]
-            + [pl.BlockSpec((rows // 2, 128), whole)] * 2
-            + [pl.BlockSpec((rows // 2, 256), whole)] * 2,
+            grid=(3 * half,),
+            in_specs=[pl.BlockSpec((128, BLOCK), at)] * 3
+            + [pl.BlockSpec((128, BLOCK), far_at)] * 3
+            + [pl.BlockSpec((BLOCK, 768), lambda s, core: (theirs(s, core), 0))]
+            + [pl.BlockSpec((128, BLOCK), lambda s, core: (0, jnp.minimum(s, 2 * half - 1)))]
+            + [fixed(384, 256), fixed(128, 384), fixed(128, 384), fixed(384, 256)],
             out_specs=[
-                pl.BlockSpec((384, block), lambda s, core: (0, jnp.clip(s - 2 * half, 0, half - 1))),
-                pl.BlockSpec((384, block), lambda s, core: (0, jnp.maximum(s - 3 * half, 0))),
+                pl.BlockSpec((BLOCK, 256), lambda s, core: (out_at(s), 0)),
+                pl.BlockSpec((128, BLOCK), lambda s, core: (0, out_at(s))),
+                fixed(384, 256),
             ],
-            scratch_shapes=[pltpu.VMEM((rows, 128), F32), pltpu.VMEM((256, rows), BF), pltpu.VMEM((128, rows), BF)],
+            scratch_shapes=[pltpu.VMEM((384, 128), F32)],
         ),
-        out_shape=[jax.ShapeDtypeStruct((384, width // 2), BF), jax.ShapeDtypeStruct((384, width // 2), F32)],
-        compiler_params=pltpu.CompilerParams(vmem_limit_bytes=48 << 20),
-        cost_estimate=pl.CostEstimate(flops=2 * rows * width * 512, bytes_accessed=6 * rows * width, transcendentals=0),
-    )(core, *xs, *cs, sd, h1, h2, ab1, ab2)
-
-
-def finish_kernel(keep, got, gate, up, low):
-    out = keep[...] + got[...].astype(F32)
-    gate[...] = out[0:128].T
-    up[...] = out[128:256].T
-    low[...] = out[256:384]
-
-
-def finish(keep, got):
-    width, block = keep.shape[1], 512
-    wide = pl.BlockSpec((384, block), lambda n: (0, n))
-    tall = pl.BlockSpec((block, 128), lambda n: (n, 0))
-    return pl.pallas_call(
-        finish_kernel,
-        grid=(width // block,),
-        out_shape=[jax.ShapeDtypeStruct((width, 128), F32)] * 2 + [jax.ShapeDtypeStruct((128, width), F32)],
-        in_specs=[wide, wide],
-        out_specs=[tall, tall, pl.BlockSpec((128, block), lambda n: (0, n))],
-        compiler_params=pltpu.CompilerParams(vmem_limit_bytes=32 << 20),
-    )(keep, got)
+        out_shape=[
+            jax.ShapeDtypeStruct((width // 2, 256), BF),
+            jax.ShapeDtypeStruct((128, width // 2), BF),
+            jax.ShapeDtypeStruct((384, 256), BF),
+        ],
+        compiler_params=pltpu.CompilerParams(vmem_limit_bytes=16 << 20),
+        cost_estimate=pl.CostEstimate(flops=768 * width * 512, bytes_accessed=4 * 768 * width, transcendentals=0),
+    )(core, *cs, xt, sd, g1, ht1, ht2, ab)
+
+
+def keep_kernel(core, *refs):
+    cs = refs[0:6]
+    xt, g1, g2, ht1, ht2, tall, low = refs[6:]
+    g = jnp.concatenate([g1[...], g2[...]], axis=0)
+    ht = jnp.concatenate([ht1[...], ht2[...]], axis=1)
+    tall[...], low[...] = products(xt, cs, g, ht)
+
+
+def keep_half(core, xt, cs, g1, g2, ht1, ht2):
+    width = cs[0].shape[1] // 2
+    steps = width // BLOCK
+    fixed = lambda *shape: pl.BlockSpec(shape, lambda s, core: (0, 0))
+    return pl.pallas_call(
+        keep_kernel,
+        grid_spec=pltpu.PrefetchScalarGridSpec(
+            num_scalar_prefetch=1,
+            grid=(steps,),
+            in_specs=[pl.BlockSpec((128, BLOCK), lambda s, core: (0, core[0] * steps + s))] * 6
+            + [pl.BlockSpec((BLOCK, 768), lambda s, core: (core[0] * steps + s, 0))]
+            + [fixed(384, 256)] * 2
+            + [fixed(128, 384)] * 2,
+            out_specs=[
+                pl.BlockSpec((BLOCK, 256), lambda s, core: (s, 0)),
+                pl.BlockSpec((128, BLOCK), lambda s, core: (0, s)),
+            ],
+        ),
+        out_shape=[jax.ShapeDtypeStruct((width, 256), F32), jax.ShapeDtypeStruct((128, width), F32)],
+        compiler_params=pltpu.CompilerParams(vmem_limit_bytes=16 << 20),
+        cost_estimate=pl.CostEstimate(flops=768 * width * 768, bytes_accessed=4 * 768 * width, transcendentals=0),
+    )(core, *cs, xt, g1, g2, ht1, ht2)
 
 
 def per_device(
@@ -315,27 +393,31 @@
 
     meta = jnp.concatenate([router_weight[:, None], initial_id.astype(BF), jnp.zeros((12, META - 2), BF)], axis=1)
     parts = first_gather(jnp.concatenate([tokens, meta], axis=1), core, at)
-    near, far = grow(parts)
+    near, far = (v[::-1] for v in grow(parts))
 
     weights = (teacher_gate, teacher_up, student_gate, student_up)
-    h_near, ab_near = forward(info, near, *weights)
+    h_near, ht_near, ab_near = forward(info, near, *weights)
     far, h_near = lax.optimization_barrier((far, h_near))
-    h_far, ab_far = forward(info, far, *weights)
+    h_far, ht_far, ab_far = forward(info, far, *weights)
     far_out = down(h_far, student_down, teacher_down)
     near_out = down(h_near, student_down, teacher_down)
 
     depth, scale = tokens.shape[1], 1.0 / math.sqrt(total)
+    xt = turn(near + far, depth)
     cotangent = []
-    for part, rows in zip(parts, shrink(near_out, far_out)):
+    for part, rows in zip(parts, shrink(near_out[::-1], far_out[::-1])):
         weight = part[:, depth : depth + 1].astype(F32)
         cotangent.append((weight * (weight * rows) * scale).astype(BF))
-    c_near, c_far = grow(cotangent)
-
-    send, keep = backward(
-        core.astype(jnp.int32).reshape(1), near + far, c_near + c_far, student_down, h_near, h_far, ab_near, ab_far
-    )
-    got = lax.ppermute(send, "dp", [(0, 1), (1, 0)])
-    return tuple(finish(keep, got))
+    c_near, c_far = (v[::-1] for v in grow(cotangent))
+
+    g_near = dhidden(c_near, student_down, ab_near)
+    c_far, g_near = lax.optimization_barrier((c_far, g_near))
+    side, cs = core.astype(jnp.int32).reshape(1), c_near + c_far
+    *send, g_far = send_half(side, xt, cs, student_down, g_near, ht_near, ht_far, ab_far)
+    tall_got, low_got = (lax.ppermute(v, "dp", [(0, 1), (1, 0)]) for v in send)
+    tall, low = keep_half(side, xt, cs, g_near, g_far, ht_near, ht_far)
+    tall, low = tall + tall_got.astype(F32), low + low_got.astype(F32)
+    return tall[:, 0:128], tall[:, 128:256], low
 
 
 def solution(mesh):

time: 218 us -> 202 us (0.927)
  starting transfers between devices: 78.2 us -> 71.9 us
  waiting for transfers between devices: 80.3 us -> 74.7 us
  Pallas kernels: 38.7 us -> 35.2 us
    ppermute x9, starting transfers between devices: 17.5 us -> 10.9 us  [hop_back(): lax.ppermute(value, AXES, [(to, own) for own, to in step_pairs(piece, ste...]
    ppermute x36, waiting for transfers between devices: 59.5 us -> 54.6 us  [hop(): return lax.ppermute(value, AXES, step_pairs(piece, step))]
    ppermute x1 -> x2, waiting for transfers between devices: 4.17 us -> 0.01 us  [per_device(): tall_got, low_got = (lax.ppermute(v, 'dp', [(0, 1), (1, 0)]) for v in send)]
    pallas_call x2 -> x4, Pallas kernels: 18.1 us -> 14.3 us  [the longest x1 4.99 us: send_half(): pl.pallas_call(functools.partial(send_kernel, half), grid_spec=pltpu.Pref...]
    ppermute x9, waiting for transfers between devices: 16.6 us -> 20 us  [hop_back(): lax.ppermute(value, AXES, [(to, own) for own, to in step_pairs(piece, ste...]
    unnamed x34 -> x22, local copies, waits for them, and re-layouts: 9.33 us -> 6.14 us
  transfers between devices with their start and end apart: 46 -> 47, of which waited for: 29 -> 30; matrix products, arithmetic and copies ran while one was open for 3% -> 4% of each run, Pallas kernels for 5% -> 10%
where the time goes in v3:
time: 202 us
  waiting for transfers between devices  74.7 us (37%)
  starting transfers between devices  71.9 us (36%)
  Pallas kernels  35.2 us (17%)
  local copies, waits for them, and re-layouts  9.76 us (5%)
  other arithmetic  8.96 us (4%)
    ppermute x36, starting transfers between devices, hop(): return lax.ppermute(value, AXES, step_pairs(piece, step))  60.4 us
    ppermute x36, waiting for transfers between devices, hop(): return lax.ppermute(value, AXES, step_pairs(piece, step))  54.6 us
    ppermute x9, waiting for transfers between devices, hop_back(): lax.ppermute(value, AXES, [(to, own) for own, to in step_pairs(piece, ste...  20 us
    pallas_call x2, Pallas kernels, forward(): pl.pallas_call(functools.partial(forward_kernel, count, steps), grid=(ste...  12.2 us
    ppermute x9, starting transfers between devices, hop_back(): lax.ppermute(value, AXES, [(to, own) for own, to in step_pairs(piece, ste...  10.9 us
    pallas_call x2, Pallas kernels, down(): pl.pallas_call(functools.partial(down_kernel, count), grid=(width // bloc...  6.49 us
    unnamed x22, local copies, waits for them, and re-layouts  6.14 us
    pallas_call x1, Pallas kernels, send_half(): pl.pallas_call(functools.partial(send_kernel, half), grid_spec=pltpu.Pref...  4.99 us
  transfers between devices with their start and end apart: 47, of which 30 were waited for; matrix products, arithmetic and copies ran while one was open for 4% of the time, Pallas kernels for 10%

profile of v3, /device:TPU:1, one launch (start us, length us, event | category | flops | bytes accessed | tf_op | source)
XLA Modules:
  0.0 201.5 jit_solution(3775961007991350087)
XLA Ops:
  3.2 4.7 %collective-permute-start = (bf16[8,5248]{1,0:T(8,128)(2,1)S(1)}, bf16[8,5248]{1,0:T(8,128)(2,1)S(1)}, u32[]{:S(2)}, u32[]{:S(2)}) collective-permute-start(bf16[8,5248]{1,0:T(8,128)(2,1)S(1)} %pad.10), channel_id=1, source_target_pairs={{0,16},{1,17},{2,18},{3,19},{4,20},{5,21},{6,22},{7,23},{8,24},{9,... | collective-permute-start | bytes 251912 | tf_op jit(solution)/shard_map/ppermute | solution.py:47
  7.9 2.8 %collective-permute-start.6 = (bf16[8,5248]{1,0:T(8,128)(2,1)S(1)}, bf16[8,5248]{1,0:T(8,128)(2,1)S(1)}, u32[]{:S(2)}, u32[]{:S(2)}) collective-permute-start(bf16[8,5248]{1,0:T(8,128)(2,1)S(1)} %pad.11), channel_id=1, source_target_pairs={{0,4},{1,5},{2,6},{3,7},{4,0},{5,1},{6,2},{7,3},{8,12},{9,13},{10,... | collective-permute-start | bytes 251912 | tf_op jit(solution)/shard_map/ppermute | solution.py:47
  11.5 2.5 %collective-permute-start.12 = (bf16[8,5248]{1,0:T(8,128)(2,1)S(1)}, bf16[8,5248]{1,0:T(8,128)(2,1)S(1)}, u32[]{:S(2)}, u32[]{:S(2)}) collective-permute-start(bf16[8,5248]{1,0:T(8,128)(2,1)S(1)} %slice_select_fusion), channel_id=1, source_target_pairs={{0,1},{1,0},{2,3},{3,2},{4,5},{5,4},{6,7},{7,6},{8,9},{9,8},{10,11... | collective-permute-start | bytes 251912 | tf_op jit(solution)/shard_map/ppermute | solution.py:47
  16.4 3.9 %collective-permute-done.13.got = bf16[16,5248]{1,0:T(8,128)(2,1)S(1)} collective-permute-done((bf16[16,5248]{1,0:T(8,128)(2,1)S(1)}, bf16[16,5248]{1,0:T(8,128)(2,1)S(1)}, u32[]{:S(2)}, u32[]{:S(2)}) %collective-permute-start.13) | collective-permute-done | bytes 167968 | tf_op jit(solution)/shard_map/ppermute | solution.py:47
  23.1 2.6 %collective-permute-start.2 = (bf16[16,5248]{1,0:T(8,128)(2,1)S(1)}, bf16[16,5248]{1,0:T(8,128)(2,1)S(1)}, u32[]{:S(2)}, u32[]{:S(2)}) collective-permute-start(bf16[16,5248]{1,0:T(8,128)(2,1)S(1)} %shard_map.175), channel_id=1, source_target_pairs={{0,1},{1,0},{2,3},{3,2},{4,5},{5,4},{6,7},{7,6},{8,9},{9,8},{10,11... | collective-permute-start | bytes 503816 | tf_op jit(solution)/shard_map/ppermute | solution.py:47
  30.1 2.7 %collective-permute-start.3 = (bf16[32,5248]{1,0:T(8,128)(2,1)S(1)}, bf16[32,5248]{1,0:T(8,128)(2,1)S(1)}, u32[]{:S(2)}, u32[]{:S(2)}) collective-permute-start(bf16[32,5248]{1,0:T(8,128)(2,1)S(1)} %pad_maximum_fusion.12), channel_id=1, source_target_pairs={{0,67},{1,66},{2,65},{3,64},{4,71},{5,70},{6,69},{7,68},{8,75},{9,... | collective-permute-start | bytes 1007624 | tf_op jit(solution)/shard_map/ppermute | solution.py:47
  34.6 2.8 %collective-permute-start.16 = (bf16[64,5248]{1,0:T(8,128)(2,1)S(1)}, bf16[64,5248]{1,0:T(8,128)(2,1)S(1)}, u32[]{:S(2)}, u32[]{:S(2)}) collective-permute-start(bf16[64,5248]{1,0:T(8,128)(2,1)S(1)} %pad_maximum_fusion.8), channel_id=1, source_target_pairs={{0,16},{1,17},{2,18},{3,19},{4,20},{5,21},{6,22},{7,23},{8,24},{9,... | collective-permute-start | bytes 2015240 | tf_op jit(solution)/shard_map/ppermute | solution.py:47
  41.9 7.0 %collective-permute-done.4 = bf16[64,5248]{1,0:T(8,128)(2,1)S(1)} collective-permute-done((bf16[64,5248]{1,0:T(8,128)(2,1)S(1)}, bf16[64,5248]{1,0:T(8,128)(2,1)S(1)}, u32[]{:S(2)}, u32[]{:S(2)}) %collective-permute-start.4) | collective-permute-done | bytes 671776 | tf_op jit(solution)/shard_map/ppermute | solution.py:47
  61.4 6.1 %shard_map.178 = (bf16[384,384]{1,0:T(8,128)(2,1)S(1)}, bf16[128,384]{1,0:T(8,128)(2,1)S(1)}, f32[384,256]{1,0:T(8,128)S(1)}) custom-call(s32[5]{0:T(128)S(1)} %pad_add_fusion.info, bf16[128,5248]{1,0:T(8,128)(2,1)S(1)} %pad_maximum_fusion.refs_0_.refs_3_, bf16[128,5248]{1,0:T(8,128)(2,1)S(1)} %pad_maximum_fusion.1.refs_1_.refs_4_, ...), custom_call_target="tpu_custom_call" | custom-call | flops 3019898880 | bytes 11796480 | tf_op jit(solution)/shard_map/pallas_call | solution.py:165
  69.6 3.8 %collective-permute-done.17.refs_2_.refs_5_ = bf16[128,5248]{1,0:T(8,128)(2,1)} collective-permute-done((bf16[128,5248]{1,0:T(8,128)(2,1)}, bf16[128,5248]{1,0:T(8,128)(2,1)}, u32[]{:S(2)}, u32[]{:S(2)}) %collective-permute-start.17) | collective-permute-done | bytes 1343520 | tf_op jit(solution)/shard_map/ppermute | solution.py:47
  73.5 6.1 %shard_map.180 = (bf16[384,384]{1,0:T(8,128)(2,1)S(1)}, bf16[128,384]{1,0:T(8,128)(2,1)S(1)}, f32[384,256]{1,0:T(8,128)S(1)}) custom-call(s32[5]{0:T(128)S(1)} %pad_add_fusion.info, bf16[128,5248]{1,0:T(8,128)(2,1)} %collective-permute-done.5.refs_0_.refs_3_, bf16[128,5248]{1,0:T(8,128)(2,1)} %collective-permute-done.11.refs_1_.refs_4_, ...), custom_call_target="tpu_custom_call" | custom-call | flops 3019898880 | bytes 11796480 | tf_op jit(solution)/shard_map/pallas_call | solution.py:165
  79.6 3.2 %shard_map.181 = (bf16[128,5120]{1,0:T(8,128)(2,1)S(1)}, bf16[128,5120]{1,0:T(8,128)(2,1)S(1)}, bf16[128,5120]{1,0:T(8,128)(2,1)S(1)}) custom-call(bf16[384,384]{1,0:T(8,128)(2,1)S(1)} %get-tuple-element.37.h_ref, bf16[128,5120]{1,0:T(8,128)(2,1)S(1)} %copy-done.6, bf16[256,5120]{1,0:T(8,128)(2,1)S(1)} %copy-done.7), custom_call_target="tpu_custom_call" | custom-call | flops 1509949440 | bytes 7864320 | tf_op jit(solution)/shard_map/pallas_call | solution.py:198
  85.5 3.3 %shard_map.179 = (bf16[128,5120]{1,0:T(8,128)(2,1)S(1)}, bf16[128,5120]{1,0:T(8,128)(2,1)S(1)}, bf16[128,5120]{1,0:T(8,128)(2,1)S(1)}) custom-call(bf16[384,384]{1,0:T(8,128)(2,1)S(1)} %get-tuple-element.32.h_ref, bf16[128,5120]{1,0:T(8,128)(2,1)S(1)} %copy-done.6, bf16[256,5120]{1,0:T(8,128)(2,1)S(1)} %copy-done.7), custom_call_target="tpu_custom_call" | custom-call | flops 1509949440 | bytes 7864320 | tf_op jit(solution)/shard_map/pallas_call | solution.py:198
  88.8 11.5 %collective-permute-done.30 = bf16[128,5120]{1,0:T(8,128)(2,1)S(1)} collective-permute-done((bf16[128,5120]{1,0:T(8,128)(2,1)S(1)}, bf16[128,5120]{1,0:T(8,128)(2,1)S(1)}, u32[]{:S(2)}, u32[]{:S(2)}) %collective-permute-start.30) | collective-permute-done | bytes 1310752 | tf_op jit(solution)/shard_map/ppermute | solution.py:51
  106.2 5.0 %collective-permute-done.31 = bf16[64,5120]{1,0:T(8,128)(2,1)S(1)} collective-permute-done((bf16[64,5120]{1,0:T(8,128)(2,1)S(1)}, bf16[64,5120]{1,0:T(8,128)(2,1)S(1)}, u32[]{:S(2)}, u32[]{:S(2)}) %collective-permute-start.31) | collective-permute-done | bytes 655392 | tf_op jit(solution)/shard_map/ppermute | solution.py:51
  122.7 2.6 %collective-permute-start.21 = (bf16[32,5120]{1,0:T(8,128)(2,1)S(1)}, bf16[32,5120]{1,0:T(8,128)(2,1)S(1)}, u32[]{:S(2)}, u32[]{:S(2)}) collective-permute-start(bf16[32,5120]{1,0:T(8,128)(2,1)S(1)} %get-tuple-element.63), channel_id=1, source_target_pairs={{0,4},{1,5},{2,6},{3,7},{4,0},{5,1},{6,2},{7,3},{8,12},{9,13},{10,... | collective-permute-start | bytes 983048 | tf_op jit(solution)/shard_map/ppermute | solution.py:47
  144.1 4.2 %collective-permute-start.40 = (bf16[32,5120]{1,0:T(8,128)(2,1)S(1)}, bf16[32,5120]{1,0:T(8,128)(2,1)S(1)}, u32[]{:S(2)}, u32[]{:S(2)}) collective-permute-start(bf16[32,5120]{1,0:T(8,128)(2,1)S(1)} %multiply_convert_fusion), channel_id=1, source_target_pairs={{0,76},{1,77},{2,78},{3,79},{4,72},{5,73},{6,74},{7,75},{8,68},{9,... | collective-permute-start | bytes 983048 | tf_op jit(solution)/shard_map/ppermute | solution.py:47
  151.4 4.8 %collective-permute-done.36 = bf16[32,5120]{1,0:T(8,128)(2,1)S(1)} collective-permute-done((bf16[32,5120]{1,0:T(8,128)(2,1)S(1)}, bf16[32,5120]{1,0:T(8,128)(2,1)S(1)}, u32[]{:S(2)}, u32[]{:S(2)}) %collective-permute-start.36) | collective-permute-done | bytes 327712 | tf_op jit(solution)/shard_map/ppermute | solution.py:47
  159.6 4.1 %collective-permute-start.41 = (bf16[64,5120]{1,0:T(8,128)(2,1)S(1)}, bf16[64,5120]{1,0:T(8,128)(2,1)S(1)}, u32[]{:S(2)}, u32[]{:S(2)}) collective-permute-start(bf16[64,5120]{1,0:T(8,128)(2,1)S(1)} %pad_maximum_fusion.11), channel_id=1, source_target_pairs={{0,16},{1,17},{2,18},{3,19},{4,20},{5,21},{6,22},{7,23},{8,24},{9,... | collective-permute-start | bytes 1966088 | tf_op jit(solution)/shard_map/ppermute | solution.py:47
  163.7 3.2 %collective-permute-done.37 = bf16[64,5120]{1,0:T(8,128)(2,1)S(1)} collective-permute-done((bf16[64,5120]{1,0:T(8,128)(2,1)S(1)}, bf16[64,5120]{1,0:T(8,128)(2,1)S(1)}, u32[]{:S(2)}, u32[]{:S(2)}) %collective-permute-start.37) | collective-permute-done | bytes 655392 | tf_op jit(solution)/shard_map/ppermute | solution.py:47
  172.1 4.7 %shard_map.183.refs_6_ = bf16[5120,768]{1,0:T(8,128)(2,1)S(1)} custom-call(bf16[128,5248]{1,0:T(8,128)(2,1)S(1)} %pad_maximum_fusion.refs_0_.refs_3_, bf16[128,5248]{1,0:T(8,128)(2,1)S(1)} %pad_maximum_fusion.1.refs_1_.refs_4_, bf16[128,5248]{1,0:T(8,128)(2,1)} %pad_maximum_fusion.2.refs_2_.refs_5_, ...), custom_call_target="tpu_custom_call" | custom-call | bytes 15728640 | tf_op jit(solution)/shard_map/pallas_call | solution.py:270
  179.0 6.3 %collective-permute-done.42.refs_3_ = bf16[128,5120]{1,0:T(8,128)(2,1)S(1)} collective-permute-done((bf16[128,5120]{1,0:T(8,128)(2,1)S(1)}, bf16[128,5120]{1,0:T(8,128)(2,1)S(1)}, u32[]{:S(2)}, u32[]{:S(2)}) %collective-permute-start.42) | collective-permute-done | bytes 1310752 | tf_op jit(solution)/shard_map/ppermute | solution.py:47
  187.3 3.0 %collective-permute-done.44.refs_5_ = bf16[128,5120]{1,0:T(8,128)(2,1)S(1)} collective-permute-done((bf16[128,5120]{1,0:T(8,128)(2,1)S(1)}, bf16[128,5120]{1,0:T(8,128)(2,1)S(1)}, u32[]{:S(2)}, u32[]{:S(2)}) %collective-permute-start.44) | collective-permute-done | bytes 1310752 | tf_op jit(solution)/shard_map/ppermute | solution.py:47
  190.4 5.0 %shard_map.184 = (bf16[2560,256]{1,0:T(8,128)(2,1)S(1)}, bf16[128,2560]{1,0:T(8,128)(2,1)S(1)}, bf16[384,256]{1,0:T(8,128)(2,1)S(1)}) custom-call(s32[1]{0:T(128)} %bitcast.core, bf16[128,5120]{1,0:T(8,128)(2,1)S(1)} %pad_maximum_fusion.3.refs_0_, bf16[128,5120]{1,0:T(8,128)(2,1)S(1)} %pad_maximum_fusion.4.refs_1_, ...), custom_call_target="tpu_custom_call" | custom-call | flops 2013265920 | bytes 15728640 | tf_op jit(solution)/shard_map/pallas_call | solution.py:316
  (163 shorter events, 94.3 us)
Async XLA Ops:
  3.2 13.1 %collective-permute-start = (bf16[8,5248]{1,0:T(8,128)(2,1)S(1)}, bf16[8,5248]{1,0:T(8,128)(2,1)S(1)}, u32[]{:S(2)}, u32[]{:S(2)}) collective-permute-start(bf16[8,5248]{1,0:T(8,128)(2,1)S(1)} %pad.10), channel_id=1, source_target_pairs={{0,16},{1,17},{2,18},{3,19},{4,20},{5,21},{6,22},{7,23},{8,24},{9,... | collective-permute-start | bytes 251912 | tf_op jit(solution)/shard_map/ppermute | solution.py:47
  7.9 8.2 %collective-permute-start.6 = (bf16[8,5248]{1,0:T(8,128)(2,1)S(1)}, bf16[8,5248]{1,0:T(8,128)(2,1)S(1)}, u32[]{:S(2)}, u32[]{:S(2)}) collective-permute-start(bf16[8,5248]{1,0:T(8,128)(2,1)S(1)} %pad.11), channel_id=1, source_target_pairs={{0,4},{1,5},{2,6},{3,7},{4,0},{5,1},{6,2},{7,3},{8,12},{9,13},{10,... | collective-permute-start | bytes 251912 | tf_op jit(solution)/shard_map/ppermute | solution.py:47
  28.1 11.6 %collective-permute-start.9 = (bf16[32,5248]{1,0:T(8,128)(2,1)S(1)}, bf16[32,5248]{1,0:T(8,128)(2,1)S(1)}, u32[]{:S(2)}, u32[]{:S(2)}) collective-permute-start(bf16[32,5248]{1,0:T(8,128)(2,1)S(1)} %pad_maximum_fusion.13), channel_id=1, source_target_pairs={{0,112},{1,113},{2,114},{3,115},{4,116},{5,117},{6,118},{7,119},{8... | collective-permute-start | bytes 1007624 | tf_op jit(solution)/shard_map/ppermute | solution.py:47
  30.1 7.9 %collective-permute-start.3 = (bf16[32,5248]{1,0:T(8,128)(2,1)S(1)}, bf16[32,5248]{1,0:T(8,128)(2,1)S(1)}, u32[]{:S(2)}, u32[]{:S(2)}) collective-permute-start(bf16[32,5248]{1,0:T(8,128)(2,1)S(1)} %pad_maximum_fusion.12), channel_id=1, source_target_pairs={{0,67},{1,66},{2,65},{3,64},{4,71},{5,70},{6,69},{7,68},{8,75},{9,... | collective-permute-start | bytes 1007624 | tf_op jit(solution)/shard_map/ppermute | solution.py:47
  34.6 17.2 %collective-permute-start.16 = (bf16[64,5248]{1,0:T(8,128)(2,1)S(1)}, bf16[64,5248]{1,0:T(8,128)(2,1)S(1)}, u32[]{:S(2)}, u32[]{:S(2)}) collective-permute-start(bf16[64,5248]{1,0:T(8,128)(2,1)S(1)} %pad_maximum_fusion.8), channel_id=1, source_target_pairs={{0,16},{1,17},{2,18},{3,19},{4,20},{5,21},{6,22},{7,23},{8,24},{9,... | collective-permute-start | bytes 2015240 | tf_op jit(solution)/shard_map/ppermute | solution.py:47
  38.0 10.9 %collective-permute-start.4 = (bf16[64,5248]{1,0:T(8,128)(2,1)S(1)}, bf16[64,5248]{1,0:T(8,128)(2,1)S(1)}, u32[]{:S(2)}, u32[]{:S(2)}) collective-permute-start(bf16[64,5248]{1,0:T(8,128)(2,1)S(1)} %pad_maximum_fusion.6), channel_id=1, source_target_pairs={{0,4},{1,5},{2,6},{3,7},{4,0},{5,1},{6,2},{7,3},{8,12},{9,13},{10,... | collective-permute-start | bytes 2015240 | tf_op jit(solution)/shard_map/ppermute | solution.py:47
  39.8 10.9 %collective-permute-start.10 = (bf16[64,5248]{1,0:T(8,128)(2,1)S(1)}, bf16[64,5248]{1,0:T(8,128)(2,1)S(1)}, u32[]{:S(2)}, u32[]{:S(2)}) collective-permute-start(bf16[64,5248]{1,0:T(8,128)(2,1)S(1)} %pad_maximum_fusion.7), channel_id=1, source_target_pairs={{0,1},{1,0},{2,3},{3,2},{4,5},{5,4},{6,7},{7,6},{8,9},{9,8},{10,11... | collective-permute-start | bytes 2015240 | tf_op jit(solution)/shard_map/ppermute | solution.py:47
  49.1 18.8 %collective-permute-start.5 = (bf16[128,5248]{1,0:T(8,128)(2,1)S(1)}, bf16[128,5248]{1,0:T(8,128)(2,1)}, u32[]{:S(2)}, u32[]{:S(2)}) collective-permute-start(bf16[128,5248]{1,0:T(8,128)(2,1)S(1)} %pad_maximum_fusion.refs_0_.refs_3_), channel_id=1, source_target_pairs={{0,76},{1,77},{2,78},{3,79},{4,72},{5,73},{6,74},{7,75},{8,68},{9,... | collective-permute-start | bytes 4030472 | tf_op jit(solution)/shard_map/ppermute | solution.py:47
  50.8 18.8 %collective-permute-start.11 = (bf16[128,5248]{1,0:T(8,128)(2,1)S(1)}, bf16[128,5248]{1,0:T(8,128)(2,1)}, u32[]{:S(2)}, u32[]{:S(2)}) collective-permute-start(bf16[128,5248]{1,0:T(8,128)(2,1)S(1)} %pad_maximum_fusion.1.refs_1_.refs_4_), channel_id=1, source_target_pairs={{0,67},{1,66},{2,65},{3,64},{4,71},{5,70},{6,69},{7,68},{8,75},{9,... | collective-permute-start | bytes 4030472 | tf_op jit(solution)/shard_map/ppermute | solution.py:47
  53.0 20.4 %collective-permute-start.17 = (bf16[128,5248]{1,0:T(8,128)(2,1)}, bf16[128,5248]{1,0:T(8,128)(2,1)}, u32[]{:S(2)}, u32[]{:S(2)}) collective-permute-start(bf16[128,5248]{1,0:T(8,128)(2,1)} %pad_maximum_fusion.2.refs_2_.refs_5_), channel_id=1, source_target_pairs={{0,112},{1,113},{2,114},{3,115},{4,116},{5,117},{6,118},{7,119},{8... | collective-permute-start | bytes 4030472 | tf_op jit(solution)/shard_map/ppermute | solution.py:47
  82.9 17.4 %collective-permute-start.30 = (bf16[128,5120]{1,0:T(8,128)(2,1)S(1)}, bf16[128,5120]{1,0:T(8,128)(2,1)S(1)}, u32[]{:S(2)}, u32[]{:S(2)}) collective-permute-start(bf16[128,5120]{1,0:T(8,128)(2,1)S(1)} %get-tuple-element.42), channel_id=1, source_target_pairs={{76,0},{77,1},{78,2},{79,3},{72,4},{73,5},{74,6},{75,7},{68,8},{69... | collective-permute-start | bytes 3932168 | tf_op jit(solution)/shard_map/ppermute | solution.py:51
  83.3 20.6 %collective-permute-start.18 = (bf16[128,5120]{1,0:T(8,128)(2,1)S(1)}, bf16[128,5120]{1,0:T(8,128)(2,1)S(1)}, u32[]{:S(2)}, u32[]{:S(2)}) collective-permute-start(bf16[128,5120]{1,0:T(8,128)(2,1)S(1)} %get-tuple-element.38), channel_id=1, source_target_pairs={{112,0},{113,1},{114,2},{115,3},{116,4},{117,5},{118,6},{119,7},{1... | collective-permute-start | bytes 3932168 | tf_op jit(solution)/shard_map/ppermute | solution.py:51
  85.1 17.0 %collective-permute-start.24 = (bf16[128,5120]{1,0:T(8,128)(2,1)S(1)}, bf16[128,5120]{1,0:T(8,128)(2,1)S(1)}, u32[]{:S(2)}, u32[]{:S(2)}) collective-permute-start(bf16[128,5120]{1,0:T(8,128)(2,1)S(1)} %get-tuple-element.40), channel_id=1, source_target_pairs={{67,0},{66,1},{65,2},{64,3},{71,4},{70,5},{69,6},{68,7},{75,8},{74... | collective-permute-start | bytes 3932168 | tf_op jit(solution)/shard_map/ppermute | solution.py:51
  100.5 10.7 %collective-permute-start.31 = (bf16[64,5120]{1,0:T(8,128)(2,1)S(1)}, bf16[64,5120]{1,0:T(8,128)(2,1)S(1)}, u32[]{:S(2)}, u32[]{:S(2)}) collective-permute-start(bf16[64,5120]{1,0:T(8,128)(2,1)S(1)} %get-tuple-element.67), channel_id=1, source_target_pairs={{4,0},{5,1},{6,2},{7,3},{0,4},{1,5},{2,6},{3,7},{12,8},{13,9},{14,... | collective-permute-start | bytes 1966088 | tf_op jit(solution)/shard_map/ppermute | solution.py:51
  102.4 10.7 %collective-permute-start.25 = (bf16[64,5120]{1,0:T(8,128)(2,1)S(1)}, bf16[64,5120]{1,0:T(8,128)(2,1)S(1)}, u32[]{:S(2)}, u32[]{:S(2)}) collective-permute-start(bf16[64,5120]{1,0:T(8,128)(2,1)S(1)} %get-tuple-element.69), channel_id=1, source_target_pairs={{1,0},{0,1},{3,2},{2,3},{5,4},{4,5},{7,6},{6,7},{9,8},{8,9},{11,10... | collective-permute-start | bytes 1966088 | tf_op jit(solution)/shard_map/ppermute | solution.py:51
  104.2 11.4 %collective-permute-start.19 = (bf16[64,5120]{1,0:T(8,128)(2,1)S(1)}, bf16[64,5120]{1,0:T(8,128)(2,1)S(1)}, u32[]{:S(2)}, u32[]{:S(2)}) collective-permute-start(bf16[64,5120]{1,0:T(8,128)(2,1)S(1)} %get-tuple-element.71), channel_id=1, source_target_pairs={{16,0},{17,1},{18,2},{19,3},{20,4},{21,5},{22,6},{23,7},{24,8},{25... | collective-permute-start | bytes 1966088 | tf_op jit(solution)/shard_map/ppermute | solution.py:51
  144.1 15.5 %collective-permute-start.40 = (bf16[32,5120]{1,0:T(8,128)(2,1)S(1)}, bf16[32,5120]{1,0:T(8,128)(2,1)S(1)}, u32[]{:S(2)}, u32[]{:S(2)}) collective-permute-start(bf16[32,5120]{1,0:T(8,128)(2,1)S(1)} %multiply_convert_fusion), channel_id=1, source_target_pairs={{0,76},{1,77},{2,78},{3,79},{4,72},{5,73},{6,74},{7,75},{8,68},{9,... | collective-permute-start | bytes 983048 | tf_op jit(solution)/shard_map/ppermute | solution.py:47
  149.6 8.6 %collective-permute-start.38 = (bf16[32,5120]{1,0:T(8,128)(2,1)S(1)}, bf16[32,5120]{1,0:T(8,128)(2,1)S(1)}, u32[]{:S(2)}, u32[]{:S(2)}) collective-permute-start(bf16[32,5120]{1,0:T(8,128)(2,1)S(1)} %multiply_convert_fusion.1), channel_id=1, source_target_pairs={{0,112},{1,113},{2,114},{3,115},{4,116},{5,117},{6,118},{7,119},{8... | collective-permute-start | bytes 983048 | tf_op jit(solution)/shard_map/ppermute | solution.py:47
  156.2 10.7 %collective-permute-start.37 = (bf16[64,5120]{1,0:T(8,128)(2,1)S(1)}, bf16[64,5120]{1,0:T(8,128)(2,1)S(1)}, u32[]{:S(2)}, u32[]{:S(2)}) collective-permute-start(bf16[64,5120]{1,0:T(8,128)(2,1)S(1)} %pad_maximum_fusion.9), channel_id=1, source_target_pairs={{0,4},{1,5},{2,6},{3,7},{4,0},{5,1},{6,2},{7,3},{8,12},{9,13},{10,... | collective-permute-start | bytes 1966088 | tf_op jit(solution)/shard_map/ppermute | solution.py:47
  158.2 10.7 %collective-permute-start.39 = (bf16[64,5120]{1,0:T(8,128)(2,1)S(1)}, bf16[64,5120]{1,0:T(8,128)(2,1)S(1)}, u32[]{:S(2)}, u32[]{:S(2)}) collective-permute-start(bf16[64,5120]{1,0:T(8,128)(2,1)S(1)} %pad_maximum_fusion.10), channel_id=1, source_target_pairs={{0,1},{1,0},{2,3},{3,2},{4,5},{5,4},{6,7},{7,6},{8,9},{9,8},{10,11... | collective-permute-start | bytes 1966088 | tf_op jit(solution)/shard_map/ppermute | solution.py:47
  159.6 12.1 %collective-permute-start.41 = (bf16[64,5120]{1,0:T(8,128)(2,1)S(1)}, bf16[64,5120]{1,0:T(8,128)(2,1)S(1)}, u32[]{:S(2)}, u32[]{:S(2)}) collective-permute-start(bf16[64,5120]{1,0:T(8,128)(2,1)S(1)} %pad_maximum_fusion.11), channel_id=1, source_target_pairs={{0,16},{1,17},{2,18},{3,19},{4,20},{5,21},{6,22},{7,23},{8,24},{9,... | collective-permute-start | bytes 1966088 | tf_op jit(solution)/shard_map/ppermute | solution.py:47
  167.1 18.3 %collective-permute-start.42 = (bf16[128,5120]{1,0:T(8,128)(2,1)S(1)}, bf16[128,5120]{1,0:T(8,128)(2,1)S(1)}, u32[]{:S(2)}, u32[]{:S(2)}) collective-permute-start(bf16[128,5120]{1,0:T(8,128)(2,1)S(1)} %pad_maximum_fusion.3.refs_0_), channel_id=1, source_target_pairs={{0,76},{1,77},{2,78},{3,79},{4,72},{5,73},{6,74},{7,75},{8,68},{9,... | collective-permute-start | bytes 3932168 | tf_op jit(solution)/shard_map/ppermute | solution.py:47
  169.0 18.3 %collective-permute-start.43 = (bf16[128,5120]{1,0:T(8,128)(2,1)S(1)}, bf16[128,5120]{1,0:T(8,128)(2,1)S(1)}, u32[]{:S(2)}, u32[]{:S(2)}) collective-permute-start(bf16[128,5120]{1,0:T(8,128)(2,1)S(1)} %pad_maximum_fusion.4.refs_1_), channel_id=1, source_target_pairs={{0,67},{1,66},{2,65},{3,64},{4,71},{5,70},{6,69},{7,68},{8,75},{9,... | collective-permute-start | bytes 3932168 | tf_op jit(solution)/shard_map/ppermute | solution.py:47
  171.8 18.6 %collective-permute-start.44 = (bf16[128,5120]{1,0:T(8,128)(2,1)S(1)}, bf16[128,5120]{1,0:T(8,128)(2,1)S(1)}, u32[]{:S(2)}, u32[]{:S(2)}) collective-permute-start(bf16[128,5120]{1,0:T(8,128)(2,1)S(1)} %pad_maximum_fusion.5.refs_2_), channel_id=1, source_target_pairs={{0,112},{1,113},{2,114},{3,115},{4,116},{5,117},{6,118},{7,119},{8... | collective-permute-start | bytes 3932168 | tf_op jit(solution)/shard_map/ppermute | solution.py:47
  (34 other events, 214.7 us)
